TPU v7x, 256 devices: a whole 4x4x8 slice. The times are simulated.
256 devices in a mesh: dp: 32 (over y, x, core), tensor: 8 (over z).
Axes of the slice: x: 4, y: 4, z: 8, core: 2. Of those that a mesh axis runs over, the one named last changes fastest.
Arguments:
- tokens: bfloat16 [24576, 2560], P('dp', 'tensor'), may hold values from -6 to 6
- w_in: bfloat16 [2560, 5120], P(None, 'tensor'), may hold values from -0.125 to 0.125
- pre_act: bfloat16 [24576, 5120], P('dp', 'tensor'), may hold values from -5 to 5
- grad_hidden: bfloat16 [24576, 5120], P('dp', 'tensor'), may hold values from -3 to 3
- err_state: float32 [32, 2560, 5120], P('dp', None, 'tensor'), may hold values from -3072 to 3072
- q_init: float32 [5120, 64], P('tensor'), may hold values from -6 to 6
Outputs:
- grad_input: bfloat16 [24576, 2560], P('dp', 'tensor')
- q_factor: float32 [5120, 64], P('tensor')
All inputs are finite; a program needn't handle non-finite values.
Results may differ from a plain program's by a relative error of at most 0.019.
Values may be sent and summed in bfloat16 or wider, within the bound.
A program may use at most 64 MiB of HBM per device.

v0:
```python
import jax
import jax.numpy as jnp
from jax import lax
from jax.sharding import PartitionSpec as P

highest = lax.Precision.HIGHEST
slope_coeff = 0.7978845608


def gelu_slope(argument):
    inside = slope_coeff * (argument + 0.044715 * argument * argument * argument)
    tangent = jnp.tanh(inside)
    return 0.5 * (1.0 + tangent) + 0.5 * argument * (1.0 - tangent * tangent) * slope_coeff * (
        1.0 + 0.134145 * argument * argument
    )


def contract_rows(left_side, right_side):
    return lax.dot_general(
        left_side,
        right_side,
        (((0,), (0,)), ((), ())),
        precision=highest,
        preferred_element_type=jnp.float32,
    )


def local(tokens, w_in, pre_act, grad_hidden, err_state, q_init):
    slopes = gelu_slope(pre_act.astype(jnp.float32))
    pre_grad = (grad_hidden.astype(jnp.float32) * slopes).astype(jnp.bfloat16)
    errors = err_state[0]
    weight_grad = lax.dot_general(
        lax.all_gather(tokens, "tensor", axis=1, tiled=True),
        pre_grad,
        (((0,), (0,)), ((), ())),
        preferred_element_type=jnp.float32,
    )
    merged = weight_grad + errors
    p_term = jnp.dot(merged, q_init, precision=highest)
    partial_value = lax.dot_general(
        pre_grad, w_in, (((1,), (1,)), ((), ())), preferred_element_type=jnp.float32
    )
    grad_input = lax.psum_scatter(
        partial_value.astype(jnp.bfloat16), "tensor", scatter_dimension=1, tiled=True
    )
    p_total = lax.psum(p_term, ("dp", "tensor"))
    p_gram = jnp.dot(p_total.T, p_total, precision=highest)
    factor_low = jnp.linalg.cholesky(p_gram)
    p_ortho = jax.scipy.linalg.solve_triangular(factor_low, p_total.T, lower=True).T
    q_term = contract_rows(merged, p_ortho)
    q_total = lax.psum(q_term.astype(jnp.bfloat16), "dp").astype(jnp.float32)
    return (grad_input, q_total / lax.axis_size("dp"))


def solution(mesh):
    return jax.shard_map(
        local,
        mesh=mesh,
        in_specs=(
            P("dp", "tensor"),
            P(None, "tensor"),
            P("dp", "tensor"),
            P("dp", "tensor"),
            P("dp", None, "tensor"),
            P("tensor", None),
        ),
        out_specs=(P("dp", "tensor"), P("tensor", None)),
        check_vma=False,
    )
```

profile of v0, /device:TPU:1, one launch (start us, length us, event | category | flops | bytes accessed | tf_op | source)
XLA Modules:
  0.0 525.0 jit_solution(7069986990637471300)
XLA Ops:
  7.2 0.0 all-gather.2.cloned.1.call-start
  7.2 0.7 all-gather.2.cloned.1.call-update
  7.9 0.0 all-reduce.3.cloned.1.call-start
  8.0 8.4 %copy.8 = f32[1,2560,640]{1,2,0:T(8,128)} copy(f32[1,2560,640]{2,1,0:T(8,128)} %param.10) | data formatting | bytes 13107200 | tf_op args[4]
  16.3 49.7 %all-gather.2.cloned.1.call-done = bf16[768,2560]{0,1:T(8,128)(2,1)} async-done(((bf16[768,320]{0,1:T(8,128)(2,1)}), bf16[768,2560]{0,1:T(8,128)(2,1)}) %all-gather.2.cloned.1.call-update) | async-done | bytes 3932176 | tf_op jit(solution)/shard_map/all_gather | solution.py:33
  66.0 8.5 %bitcast_add_fusion = f32[2560,640]{0,1:T(8,128)S(1)} fusion(f32[1,2560,640]{1,2,0:T(8,128)} %copy.8, bf16[768,2560]{0,1:T(8,128)(2,1)} %all-gather.2.cloned.1.call-done, bf16[768,640]{1,0:T(8,128)(2,1)} %param.8, bf16[768,640]{1,0:T(8,128)(2,1)} %param.9), kind=kOutput, calls=%fused_computation | convolution fusion | flops 2528542720 | bytes 19005440 | tf_op jit(solution)/shard_map/dot_general | solution.py:32
  74.6 2.7 copy-done.1
  77.3 5.2 fusion.15
  82.5 0.0 all-reduce.3.cloned.1.call-update
  82.5 0.2 all-reduce.5.cloned.1.call-start
  82.7 250.1 %all-reduce.3.cloned.1.call-done = f32[2560,64]{0,1:T(8,128)} async-done(((f32[2560,64]{0,1:T(8,128)}), f32[2560,64]{0,1:T(8,128)}) %all-reduce.3.cloned.1.call-update) | async-done | bytes 655376 | tf_op jit(solution)/shard_map/psum | solution.py:46
  332.8 2.0 fusion.16
  334.8 0.1 copy.9
  334.9 5.8 %cholesky.16 = f32[64,64]{1,0:T(8,128)S(1)} custom-call(f32[64,64]{1,0:T(8,128)S(1)} %fusion.12), custom_call_target="Cholesky" | custom-call | tf_op jit(solution)/shard_map/jit(cholesky)/cholesky | solution.py:48
  340.8 0.6 compare_reduce_fusion
  341.4 0.7 fusion.9
  342.1 4.9 custom-call.7
  347.0 1.8 fusion.10
  348.8 9.0 %convolution_convert_fusion.1 = bf16[640,64]{0,1:T(8,128)(2,1)} fusion(f32[2560,640]{0,1:T(8,128)} %copy-done.1, f32[64,2560]{1,0:T(8,128)S(1)} %fusion.10), kind=kOutput, calls=%fused_computation.18 | convolution fusion | flops 1258332160 | bytes 7290880 | tf_op jit(solution)/shard_map/dot_general | solution.py:19
  357.8 0.0 reduce-scatter.2.cloned.1.call-start
  357.8 7.3 %convolution_convert_fusion = bf16[768,2560]{0,1:T(8,128)(2,1)} fusion(bf16[2560,640]{1,0:T(8,128)(2,1)S(1)} %copy-done, bf16[768,640]{1,0:T(8,128)(2,1)} %param.8, bf16[768,640]{1,0:T(8,128)(2,1)} %param.9), kind=kOutput, calls=%fused_computation.1 | convolution fusion | flops 2528870400 | bytes 9175040 | tf_op jit(solution)/shard_map/dot_general | solution.py:40
  365.2 98.5 %all-reduce.5.cloned.1.call-done = bf16[640,64]{0,1:T(8,128)(2,1)} async-done(((bf16[640,64]{0,1:T(8,128)(2,1)}), bf16[640,64]{0,1:T(8,128)(2,1)}) %all-reduce.5.cloned.1.call-update) | async-done | bytes 81936 | tf_op jit(solution)/shard_map/psum | solution.py:51
  463.7 1.6 convert_multiply_fusion.6
  465.3 53.2 %reduce-scatter.2.cloned.1.call-done = bf16[768,320]{0,1:T(8,128)(2,1)} async-done(((bf16[768,2560]{0,1:T(8,128)(2,1)}), bf16[768,320]{0,1:T(8,128)(2,1)}) %reduce-scatter.2.cloned.1.call-update) | async-done | bytes 491536 | tf_op jit(solution)/shard_map/reduce_scatter | solution.py:43
  (9 shorter events, 0.1 us)
Async XLA Ops:
  7.2 350.7 %copy-start = (bf16[2560,640]{1,0:T(8,128)(2,1)S(1)}, bf16[2560,640]{1,0:T(8,128)(2,1)}, u32[]{:S(2)}) copy-start(bf16[2560,640]{1,0:T(8,128)(2,1)} %param.7) | copy-start | bytes 9830404
  7.2 58.8 %all-gather.2.cloned.1.call-start = ((), (), s32[]{:S(2)}) async-start(), calls=%async_computation.2 | async-start | bytes 4423680 | tf_op jit(solution)/shard_map/all_gather | solution.py:33
  7.9 324.9 %all-reduce.3.cloned.1.call-start = ((), (), s32[]{:S(2)}) async-start(), calls=%async_computation.3 | async-start | bytes 1310720 | tf_op jit(solution)/shard_map/psum | solution.py:46
  16.3 61.0 %copy-start.2 = (f32[640,64]{0,1:T(8,128)S(1)}, f32[640,64]{0,1:T(8,128)}, u32[]{:S(2)}) copy-start(f32[640,64]{0,1:T(8,128)} %param.11) | copy-start | bytes 491524
  74.6 2.7 copy-start.1
  82.5 381.2 %all-reduce.5.cloned.1.call-start = ((), (), s32[]{:S(2)}) async-start(), calls=%async_computation.4 | async-start | bytes 163840 | tf_op jit(solution)/shard_map/psum | solution.py:51
  357.8 160.7 %reduce-scatter.2.cloned.1.call-start = ((), (), s32[]{:S(2)}) async-start(), calls=%async_computation.1 | async-start | bytes 4423680 | tf_op jit(solution)/shard_map/reduce_scatter | solution.py:43
Sparse Core Ops, SparseCore 0:
  9.8 56.1 all-gather.1
  82.6 250.1 all-reduce.2
  357.9 105.7 all-reduce.4
  466.7 51.7 reduce-scatter.1
where the time goes:
time: 525 us
  waiting for transfers between devices  452 us (86%)
  matrix products  33.8 us (6%)
  between operations  13.8 us (3%)
  other arithmetic  13.6 us (3%)
  local copies, waits for them, and re-layouts  11.2 us (2%)
    psum x1, waiting for transfers between devices, local(): p_total = lax.psum(p_term, ('dp', 'tensor'))  250 us
    psum x1, waiting for transfers between devices, local(): q_total = lax.psum(q_term.astype(jnp.bfloat16), 'dp').astype(jnp.float32)  98.5 us
    reduce_scatter x1, waiting for transfers between devices, local(): lax.psum_scatter(partial_value.astype(jnp.bfloat16), 'tensor', scatter_di...  53.2 us
    all_gather x1, waiting for transfers between devices, local(): lax.all_gather(tokens, 'tensor', axis=1, tiled=True)  49.7 us
    unnamed x7, local copies, waits for them, and re-layouts  11.1 us
  transfers between devices with their start and end apart: 4, of which 4 were waited for; matrix products, arithmetic and copies ran while one was open for 3% of the time, Pallas kernels for 0%

commit v1 on v0

v1 whole, which is shorter than its diff:
```python
import jax
import jax.numpy as jnp
from jax import lax
from jax.experimental import pallas as pl
from jax.experimental.pallas import tpu as pltpu
from jax.sharding import PartitionSpec as P

highest = lax.Precision.HIGHEST
slope_coeff = 0.7978845608
MESH = pl.DeviceIdType.MESH
F32, BF16 = jnp.float32, jnp.bfloat16
NX, NY, NZ = 4, 4, 8
R, TOK, FEAT, HID = 64, 768, 320, 640
NN = (((1,), (0,)), ((), ()))
NT = (((1,), (1,)), ((), ()))


def gelu_slope(argument):
    inside = slope_coeff * (argument + 0.044715 * argument * argument * argument)
    tangent = jnp.tanh(inside)
    return 0.5 * (1.0 + tangent) + 0.5 * argument * (1.0 - tangent * tangent) * slope_coeff * (
        1.0 + 0.134145 * argument * argument
    )


def halves(value):
    high = value.astype(BF16)
    return high, (value - high.astype(F32)).astype(BF16)


def dot(left, right, dims):
    return lax.dot_general(left, right, dims, preferred_element_type=F32)


def dot_wide(left, right, dims):
    rows = left.shape[0]
    both = dot(jnp.concatenate(halves(left), axis=0), right, dims)
    return both[:rows] + both[rows:]


def dot_wide2(left, right, dims):
    high, low = halves(right)
    return dot_wide(left, high, dims) + dot(left.astype(BF16), low, dims)


def inverse_factor(gram, work):
    row_id = lax.broadcasted_iota(jnp.int32, (R, R), 0)
    col_id = lax.broadcasted_iota(jnp.int32, (R, R), 1)
    eye = (row_id == col_id).astype(F32)
    work[...] = jnp.concatenate([gram, eye], axis=1)
    lane = lax.broadcasted_iota(jnp.int32, (1, 2 * R), 1)
    below = lax.broadcasted_iota(jnp.int32, (R, 1), 0)

    def step(k, carry):
        row = work[pl.ds(k, 1), :]
        here = lane == k
        pivot = jnp.sum(jnp.where(here, row, 0.0), axis=1, keepdims=True)
        whole = work[...]
        column = jnp.sum(jnp.where(here, whole, 0.0), axis=1, keepdims=True)
        ratio = jnp.where(below > k, column / pivot, 0.0)
        work[...] = whole - ratio * row
        return carry

    lax.fori_loop(0, R, step, 0)
    diag = jnp.sum(work[:, :R] * eye, axis=1, keepdims=True)
    return work[:, R:] * lax.rsqrt(diag)


def chain_kernel(
    xt, g, e, qt, out,
    h_part, h_rs, h_ag, z_part, z_rs, z_ag,
    px_part, px_c, px_x, px_y, px_row, pt,
    pe_part, pe_c, pe_x, pe_z, pf,
    y_part, y_c, y_x, y_y, y_f, work,
    s_z, r_z, s_x, r_x, s_y, r_y, s_c, r_c,
):
    dp, z = lax.axis_index("dp"), lax.axis_index("tensor")
    c, x, y = lax.rem(dp, 2), lax.rem(dp // 2, NX), dp // (2 * NX)
    o = 1 - c

    def at(yy, xx, cc, zz):
        return ((yy * NX + xx) * 2 + cc, zz)

    axes = {
        "z": (NZ, z, lambda j: at(y, x, c, j), s_z, r_z),
        "x": (NX, x, lambda j: at(y, j, c, z), s_x, r_x),
        "y": (NY, y, lambda j: at(j, x, c, z), s_y, r_y),
    }
    sent = []

    def start(axis, phase, src, dst):
        n, me, dev, ss, rs = axes[axis]
        for k in range(1, n):
            j = lax.rem(me + k, n)
            cp = pltpu.make_async_remote_copy(
                src_ref=src(j), dst_ref=dst(me), send_sem=ss.at[phase, k], recv_sem=rs.at[phase, me],
                device_id=dev(j), device_id_type=MESH)
            cp.start()
            sent.append(cp)

    def finish(axis, phase, dst):
        n, me, dev, ss, rs = axes[axis]
        for k in range(1, n):
            j = lax.rem(me + k, n)
            pltpu.make_async_remote_copy(
                src_ref=dst(j), dst_ref=dst(j), send_sem=ss.at[phase, k], recv_sem=rs.at[phase, j],
                device_id=dev(j), device_id_type=MESH).wait_recv()

    def swap(phase, src, dst):
        cp = pltpu.make_async_remote_copy(
            src_ref=src, dst_ref=dst, send_sem=s_c.at[phase], recv_sem=r_c.at[phase],
            device_id=at(y, x, o, z), device_id_type=MESH)
        cp.start()
        sent.append(cp)

    def swapped(phase, dst):
        pltpu.make_async_remote_copy(
            src_ref=dst, dst_ref=dst, send_sem=s_c.at[phase], recv_sem=r_c.at[phase],
            device_id=at(y, x, o, z), device_id_type=MESH).wait_recv()

    barrier = pltpu.get_barrier_semaphore()
    for axis in "zxy":
        n, me, dev = axes[axis][:3]
        for k in range(1, n):
            pl.semaphore_signal(barrier, inc=1, device_id=dev(lax.rem(me + k, n)), device_id_type=MESH)
    pl.semaphore_signal(barrier, inc=1, device_id=at(y, x, o, z), device_id_type=MESH)

    h_part[...] = dot_wide(qt[...], g[...], NT).reshape(NZ, 8, TOK)
    pl.semaphore_wait(barrier, 14)
    start("z", 0, lambda j: h_part.at[j], lambda i: h_rs.at[i])
    h_rs[z] = h_part[z]

    def error_rows(t, carry):
        rows = e[pl.ds(pl.multiple_of(t * FEAT, FEAT), FEAT), :]
        pe_part[:, :, t] = dot_wide2(qt[...], rows, NT).reshape(2, NX, 8, FEAT)
        return carry

    lax.fori_loop(0, NZ, error_rows, 0)
    swap(0, pe_part.at[o], pe_c)

    finish("z", 0, lambda i: h_rs.at[i])
    h_ag[z] = jnp.sum(h_rs[...], axis=0)
    start("z", 1, lambda j: h_ag.at[z], lambda i: h_ag.at[i])

    swapped(0, pe_c)
    pe_c[...] += pe_part[c]
    start("x", 0, lambda j: pe_c.at[j], lambda i: pe_x.at[i])
    pe_x[x] = pe_c[x]

    finish("z", 1, lambda i: h_ag.at[i])
    px_part[...] = dot_wide(h_ag[...].reshape(R, TOK), xt[...], NT).reshape(2, NX, 8, FEAT)
    swap(1, px_part.at[o], px_c)

    finish("x", 0, lambda i: pe_x.at[i])
    pe_x[x] = pe_x[0] + pe_x[1] + pe_x[2] + pe_x[3]
    start("z", 2, lambda j: pe_x.at[x, j], lambda i: pe_z.at[i])
    pe_z[z] = pe_x[x, z]

    swapped(1, px_c)
    px_c[...] += px_part[c]
    start("x", 1, lambda j: px_c.at[j], lambda i: px_x.at[i])
    px_x[x] = px_c[x]
    finish("x", 1, lambda i: px_x.at[i])
    finish("z", 2, lambda i: pe_z.at[i])
    px_y[y] = jnp.sum(px_x[...], axis=0) + jnp.sum(pe_z[...], axis=0)
    start("y", 0, lambda j: px_y.at[y], lambda i: px_y.at[i])
    finish("y", 0, lambda i: px_y.at[i])
    p_row = jnp.sum(px_y[...], axis=0)
    pt[c, x] = p_row
    pf[c, x, z] = p_row
    start("x", 2, lambda j: pt.at[c, x], lambda i: pt.at[c, i])
    start("z", 3, lambda j: pf.at[c, x, z], lambda i: pf.at[c, x, i])
    finish("x", 2, lambda i: pt.at[c, i])
    swap(2, pt.at[c], pt.at[c])
    swapped(2, pt.at[o])

    z_part[...] = dot_wide(pt[...].reshape(R, FEAT), xt[...], NN).reshape(NZ, 8, TOK)
    start("z", 4, lambda j: z_part.at[j], lambda i: z_rs.at[i])
    z_rs[z] = z_part[z]

    finish("z", 3, lambda i: pf.at[c, x, i])
    start("x", 3, lambda j: pf.at[c, x], lambda i: pf.at[c, i])

    finish("z", 4, lambda i: z_rs.at[i])
    z_ag[z] = jnp.sum(z_rs[...], axis=0)
    start("z", 5, lambda j: z_ag.at[z], lambda i: z_ag.at[i])

    finish("x", 3, lambda i: pf.at[c, i])
    swap(3, pf.at[c], pf.at[c])
    swapped(3, pf.at[o])

    def features(t, carry):
        gram, total = carry
        block = pf[:, :, t].reshape(R, FEAT)
        rows = e[pl.ds(pl.multiple_of(t * FEAT, FEAT), FEAT), :]
        gram += lax.dot_general(block, block, NT, precision=highest, preferred_element_type=F32)
        return gram, total + dot_wide2(block, rows, NN)

    gram, y_err = lax.fori_loop(0, NZ, features, (jnp.zeros((R, R), F32), jnp.zeros((R, HID), F32)))

    finish("z", 5, lambda i: z_ag.at[i])
    y_part[...] = (y_err + dot_wide(z_ag[...].reshape(R, TOK), g[...], NN)).reshape(2, NX, 8, HID)
    swap(4, y_part.at[o], y_c)
    inverse = inverse_factor(gram, work)
    swapped(4, y_c)
    y_c[...] += y_part[c]
    start("x", 4, lambda j: y_c.at[j], lambda i: y_x.at[i])
    y_x[x] = y_c[x]
    finish("x", 4, lambda i: y_x.at[i])
    y_y[y] = jnp.sum(y_x[...], axis=0)
    start("y", 1, lambda j: y_y.at[y], lambda i: y_y.at[i])
    finish("y", 1, lambda i: y_y.at[i])
    y_f[c, x] = jnp.sum(y_y[...], axis=0)
    start("x", 5, lambda j: y_f.at[c, x], lambda i: y_f.at[c, i])
    finish("x", 5, lambda i: y_f.at[c, i])
    swap(5, y_f.at[c], y_f.at[c])
    swapped(5, y_f.at[o])
    out[...] = lax.dot_general(
        inverse, y_f[...].reshape(R, HID), NN, precision=highest, preferred_element_type=F32
    ) * (1.0 / (NX * NY * 2))
    for cp in sent:
        cp.wait_send()


def chain(xt, g, e, qt):
    vm = lambda *shape: pltpu.VMEM(shape, F32)
    dma = pltpu.SemaphoreType.DMA
    spec = pl.BlockSpec(memory_space=pltpu.VMEM)
    return pl.pallas_call(
        chain_kernel,
        out_shape=jax.ShapeDtypeStruct((R, HID), F32),
        in_specs=[spec] * 4,
        out_specs=spec,
        scratch_shapes=[vm(NZ, 8, TOK)] * 6
        + [vm(2, NX, 8, FEAT), vm(NX, 8, FEAT), vm(NX, 8, FEAT), vm(NY, 8, FEAT), vm(8, FEAT), vm(2, NX, 8, FEAT)]
        + [vm(2, NX, NZ, 8, FEAT), vm(NX, NZ, 8, FEAT), vm(NX, NZ, 8, FEAT), vm(NZ, 8, FEAT), vm(2, NX, NZ, 8, FEAT)]
        + [vm(2, NX, 8, HID), vm(NX, 8, HID), vm(NX, 8, HID), vm(NY, 8, HID), vm(2, NX, 8, HID), vm(R, 2 * R)]
        + [dma((6, NZ)), dma((6, NZ)), dma((6, NX)), dma((6, NX)), dma((2, NY)), dma((2, NY)), dma((6,)), dma((6,))],
        compiler_params=pltpu.CompilerParams(
            collective_id=0, has_side_effects=True, vmem_limit_bytes=48 << 20),
        cost_estimate=pl.CostEstimate(flops=10**9, bytes_accessed=100 * 10**6, transcendentals=0),
        name="chain",
    )(xt, g, e, qt)


def local(tokens, w_in, pre_act, grad_hidden, err_state, q_init):
    slopes = gelu_slope(pre_act.astype(F32))
    pre_grad = (grad_hidden.astype(F32) * slopes).astype(BF16)
    partial_value = dot(w_in, pre_grad, NT)
    grad_input = lax.psum_scatter(partial_value.astype(BF16), "tensor", scatter_dimension=0, tiled=True)
    q_factor = chain(tokens.T, pre_grad, err_state[0], q_init.T)
    return (grad_input.T, q_factor.T)


def solution(mesh):
    return jax.shard_map(
        local,
        mesh=mesh,
        in_specs=(
            P("dp", "tensor"),
            P(None, "tensor"),
            P("dp", "tensor"),
            P("dp", "tensor"),
            P("dp", None, "tensor"),
            P("tensor", None),
        ),
        out_specs=(P("dp", "tensor"), P("tensor", None)),
        check_vma=False,
    )
```

time: 525 us -> 120 us (0.23)
  waiting for transfers between devices: 452 us -> 0.04 us
  Pallas kernels: 0 us -> 86.7 us
  matrix products: 33.8 us -> 4.81 us
  other arithmetic: 13.6 us -> 3.02 us
    psum x2 -> x0, waiting for transfers between devices: 349 us -> none  [the longest x1 250 us: local(): p_total = lax.psum(p_term, ('dp', 'tensor'))]
    pallas_call x0 -> x1, Pallas kernels: none -> 86.7 us  [chain(): pl.pallas_call(chain_kernel, out_shape=jax.ShapeDtypeStruct((R, HID), F32...]
    reduce_scatter x1 -> x0, waiting for transfers between devices: 53.2 us -> none  [local(): lax.psum_scatter(partial_value.astype(jnp.bfloat16), 'tensor', scatter_di...]
    all_gather x1 -> x0, waiting for transfers between devices: 49.7 us -> none  [local(): lax.all_gather(tokens, 'tensor', axis=1, tiled=True)]
    dot_general x5 -> x1, matrix products: 32 us -> 4.81 us  [dot(): return lax.dot_general(left, right, dims, preferred_element_type=F32)]
    another operation x5 -> x0, other arithmetic: 12.1 us -> none  [the longest x3 6.52 us: local(): factor_low = jnp.linalg.cholesky(p_gram)]
    unnamed x7 -> x12, local copies, waits for them, and re-layouts: 11.1 us -> 11.1 us
  transfers between devices with their start and end apart: 4 -> 1, of which waited for: 4 -> 0; matrix products, arithmetic and copies ran while one was open for 3% -> 0% of each run, Pallas kernels for 0% -> 72%
where the time goes in v1:
time: 120 us
  Pallas kernels  86.7 us (72%)
  between operations  14.1 us (12%)
  local copies, waits for them, and re-layouts  11.1 us (9%)
  matrix products  4.81 us (4%)
  other arithmetic  3.02 us (3%)
    pallas_call x1, Pallas kernels, chain(): pl.pallas_call(chain_kernel, out_shape=jax.ShapeDtypeStruct((R, HID), F32...  86.7 us
    unnamed x12, local copies, waits for them, and re-layouts  11.1 us
    dot_general x1, matrix products, dot(): return lax.dot_general(left, right, dims, preferred_element_type=F32)  4.81 us
    convert_element_type x1, other arithmetic, local(): pre_grad = (grad_hidden.astype(F32) * slopes).astype(BF16)  3.02 us
  transfers between devices with their start and end apart: 1, of which 0 were waited for; matrix products, arithmetic and copies ran while one was open for 0% of the time, Pallas kernels for 72%

profile of v1, /device:TPU:1, one launch (start us, length us, event | category | flops | bytes accessed | tf_op | source)
XLA Modules:
  0.0 119.8 jit_solution(8976354309002157027)
XLA Ops:
  7.2 0.0 copy-start
  7.2 0.0 reduce-scatter.4.cloned.1.call-start
  7.2 3.0 %fusion.8.g = bf16[768,640]{1,0:T(8,128)(2,1)S(1)} fusion(bf16[768,640]{1,0:T(8,128)(2,1)} %param.8, bf16[768,640]{1,0:T(8,128)(2,1)} %param.9), kind=kLoop, calls=%fused_computation.16 | loop fusion | flops 10321920 | bytes 2949120 | tf_op jit(solution)/shard_map/convert_element_type | solution.py:248
  10.2 0.0 copy-done
  10.3 4.8 %fusion = bf16[2560,768]{0,1:T(8,128)(2,1)} fusion(bf16[768,640]{1,0:T(8,128)(2,1)S(1)} %fusion.8.g, bf16[2560,640]{1,0:T(8,128)(2,1)S(1)} %copy-done), kind=kOutput, calls=%fused_computation.8 | convolution fusion | flops 2518548480 | bytes 8192000 | tf_op jit(solution)/shard_map/dot_general | solution.py:32
  15.1 0.0 copy-start.1
  15.1 1.1 copy-done.1
  16.1 6.3 %copy.10 = bf16[2560,768]{1,0:T(8,128)(2,1)} copy(bf16[2560,768]{0,1:T(8,128)(2,1)} %fusion) | data formatting | bytes 7864320
  22.4 0.0 reduce-scatter.4.cloned.1.call-update
  22.4 0.0 copy-start.2
  22.4 1.2 copy-done.2
  23.6 0.0 copy-start.3
  23.6 1.0 copy-done.3
  24.6 0.0 copy-start.4
  24.6 0.9 copy-done.4
  25.6 86.7 %chain.1 = f32[64,640]{1,0:T(8,128)S(1)} custom-call(bf16[320,768]{1,0:T(8,128)(2,1)S(1)} %bitcast.12, bf16[768,640]{1,0:T(8,128)(2,1)S(1)} %copy-done.2, f32[2560,640]{1,0:T(8,128)} %bitcast.14, f32[64,640]{1,0:T(8,128)S(1)} %bitcast.13), custom_call_target="tpu_custom_call" | custom-call | flops 1000000000 | bytes 100000000 | tf_op jit(solution)/shard_map/chain/pallas_call | solution.py:229
  112.3 0.0 reduce-scatter.4.cloned.1.call-done
  112.3 0.7 copy.14
Async XLA Ops:
  7.2 3.1 %copy-start = (bf16[2560,640]{1,0:T(8,128)(2,1)S(1)}, bf16[2560,640]{1,0:T(8,128)(2,1)}, u32[]{:S(2)}) copy-start(bf16[2560,640]{1,0:T(8,128)(2,1)} %param.7) | copy-start | bytes 9830404
  7.2 105.1 %reduce-scatter.4.cloned.1.call-start = ((), (), s32[]{:S(2)}) async-start(), calls=%async_computation.1 | async-start | bytes 4423680
  15.1 1.1 copy-start.1
  22.4 1.2 %copy-start.2 = (bf16[768,640]{1,0:T(8,128)(2,1)S(1)}, bf16[768,640]{1,0:T(8,128)(2,1)}, u32[]{:S(2)}) copy-start(bf16[768,640]{1,0:T(8,128)(2,1)} %copy-done.1) | copy-start | bytes 2949124
  23.6 1.0 copy-start.3
  24.6 0.9 copy-start.4
Sparse Core Ops, SparseCore 0:
  22.5 75.4 reduce-scatter.3

commit v2 on v1

v2 whole, which is shorter than its diff:
```python
import jax
import jax.numpy as jnp
from jax import lax
from jax.experimental import pallas as pl
from jax.experimental.pallas import tpu as pltpu
from jax.sharding import PartitionSpec as P

highest = lax.Precision.HIGHEST
slope_coeff = 0.7978845608
MESH = pl.DeviceIdType.MESH
F32, BF16 = jnp.float32, jnp.bfloat16
NX, NY, NZ = 4, 4, 8
R, TOK, FEAT, HID = 64, 768, 320, 640
NCH = 2
HALF = FEAT // 2
CHUNK = HALF // NCH
HOPS = (4, 3, 3, 2, 2, 1, 1)
NN = (((1,), (0,)), ((), ()))
NT = (((1,), (1,)), ((), ()))


def gelu_slope(argument):
    square = argument * argument
    tangent = jnp.tanh(argument * (slope_coeff + (slope_coeff * 0.044715) * square))
    linear = argument * (slope_coeff + (slope_coeff * 0.134145) * square)
    return 0.5 * (1.0 + tangent) * (1.0 + (1.0 - tangent) * linear)


def halves(value):
    high = value.astype(BF16)
    return high, (value - high.astype(F32)).astype(BF16)


def dot(left, right, dims):
    return lax.dot_general(left, right, dims, preferred_element_type=F32)


def dot_wide(left, right, dims):
    rows = left.shape[0]
    both = dot(jnp.concatenate(halves(left), axis=0), right, dims)
    return both[:rows] + both[rows:]


def dot_wide2(left, right, dims):
    high, low = halves(right)
    return dot_wide(left, high, dims) + dot(left.astype(BF16), low, dims)


def pair_rows(value):
    n = value.shape[-1] // 2
    return jnp.concatenate([value[..., :n], value[..., n:]], axis=-2)


def unpair_rows(value):
    return jnp.concatenate([value[..., :8, :], value[..., 8:, :]], axis=-1)


def eliminate(work, first, last):
    whole = work[...]
    below = lax.broadcasted_iota(jnp.int32, (R, 1), 0)
    for k in range(first, last):
        row = whole[k:k + 1, :]
        column = whole[:, k:k + 1]
        ratio = jnp.where(below > k, column / whole[k:k + 1, k:k + 1], 0.0)
        whole = whole - ratio * row
    work[...] = whole


def kernel(
    pre_hbm, gh_hbm, qt_hbm, w_hbm, e_hbm, xt_hbm, q_out, gi_out,
    pre, gh, qt, w, e, xt, g, part, ring,
    h_part, h_rs, h_ag, z_part, z_rs, z_ag,
    px_part, px_c, px_x, px_y, pt,
    pe_part, pe_c, pe_x, pe_z, pf,
    y_part, y_c, y_x, y_y, y_f, y_err, work,
    s_z, r_z, s_x, r_x, s_y, r_y, s_c, r_c, s_g, r_g, s_in,
):
    dp, z = lax.axis_index("dp"), lax.axis_index("tensor")
    c, x, y = lax.rem(dp, 2), lax.rem(dp // 2, NX), dp // (2 * NX)
    o = 1 - c

    def at(yy, xx, cc, zz):
        return ((yy * NX + xx) * 2 + cc, zz)

    axes = {
        "z": (NZ, z, lambda j: at(y, x, c, j), s_z, r_z),
        "x": (NX, x, lambda j: at(y, j, c, z), s_x, r_x),
        "y": (NY, y, lambda j: at(j, x, c, z), s_y, r_y),
    }
    sent = []

    def remote(src, dst, ss, rs, dev):
        return pltpu.make_async_remote_copy(
            src_ref=src, dst_ref=dst, send_sem=ss, recv_sem=rs, device_id=dev, device_id_type=MESH)

    def push(src, dst, ss, rs, dev):
        cp = remote(src, dst, ss, rs, dev)
        cp.start()
        sent.append(cp)

    def start(axis, phase, src, dst):
        n, me, dev, ss, rs = axes[axis]
        for k in range(1, n):
            j = lax.rem(me + k, n)
            push(src(j), dst(me), ss.at[phase, k], rs.at[phase, me], dev(j))

    def finish(axis, phase, dst):
        n, me, dev, ss, rs = axes[axis]
        for k in range(1, n):
            j = lax.rem(me + k, n)
            remote(dst(j), dst(j), ss.at[phase, k], rs.at[phase, j], dev(j)).wait_recv()

    def swap(phase, src, dst):
        push(src, dst, s_c.at[phase], r_c.at[phase], at(y, x, o, z))

    def swapped(phase, dst):
        remote(dst, dst, s_c.at[phase], r_c.at[phase], at(y, x, o, z)).wait_recv()

    def shifted(direction, hops):
        return lax.rem(z + (hops if direction == 0 else NZ - hops), NZ)

    def piece(direction, m, ch):
        half = (direction + m) % 2
        return pl.ds(half * HALF + ch * CHUNK, CHUNK)

    def ring_send(direction, m, ch, src):
        push(src, ring.at[direction, m, ch], s_g.at[direction, m, ch], r_g.at[direction, m, ch],
             at(y, x, c, shifted(direction, 1)))

    def ring_first(direction, m):
        for ch in range(NCH):
            ring_send(direction, m, ch, part.at[shifted(direction, HOPS[m]), piece(direction, m, ch)])

    def ring_wait(direction, m, ch):
        slot = ring.at[direction, m, ch]
        remote(slot, slot, s_g.at[direction, m, ch], r_g.at[direction, m, ch],
               at(y, x, c, shifted(direction, 1))).wait_recv()

    def ring_event(m, ch):
        for direction in range(2):
            ring_wait(direction, m, ch)
            if m < 5:
                own = part[shifted(direction, HOPS[m + 2]), piece(direction, m, ch)]
                ring[direction, m, ch] = (ring[direction, m, ch].astype(F32) + own.astype(F32)).astype(BF16)
                ring_send(direction, m + 2, ch, ring.at[direction, m, ch])

    events = [(m, ch) for m in range(7) for ch in range(NCH)]

    def pump(count):
        for _ in range(count):
            if events:
                ring_event(*events.pop(0))

    def product(t):
        rows = w[pl.ds(pl.multiple_of(t * FEAT, FEAT), FEAT), :]
        part[t] = dot(rows, g[...], NT).astype(BF16)

    loads = [
        pltpu.make_async_copy(src, dst, s_in.at[i])
        for i, (src, dst) in enumerate(
            [(pre_hbm, pre), (gh_hbm, gh), (qt_hbm, qt), (w_hbm, w), (e_hbm, e), (xt_hbm, xt)])
    ]
    for cp in loads:
        cp.start()
    barrier = pltpu.get_barrier_semaphore()
    for axis in "zxy":
        n, me, dev = axes[axis][:3]
        for k in range(1, n):
            pl.semaphore_signal(barrier, inc=1, device_id=dev(lax.rem(me + k, n)), device_id_type=MESH)
    pl.semaphore_signal(barrier, inc=1, device_id=at(y, x, o, z), device_id_type=MESH)

    loads[0].wait()
    loads[1].wait()

    def activate(i, carry):
        rows = pl.ds(pl.multiple_of(i * 64, 64), 64)
        g[rows, :] = (gh[rows, :].astype(F32) * gelu_slope(pre[rows, :].astype(F32))).astype(BF16)
        return carry

    lax.fori_loop(0, TOK // 64, activate, 0)
    loads[2].wait()
    h_part[...] = pair_rows(dot_wide(qt[...], g[...], NT).reshape(NZ, 8, TOK)).astype(BF16)
    pl.semaphore_wait(barrier, 14)
    start("z", 0, lambda j: h_part.at[j], lambda i: h_rs.at[i])
    h_rs[z] = h_part[z]

    loads[3].wait()
    product(shifted(0, 4))
    ring_first(0, 0)
    ring_first(1, 0)
    product(shifted(0, 3))
    ring_first(0, 1)
    product(shifted(1, 3))
    ring_first(1, 1)

    loads[4].wait()

    def error_rows(t, carry):
        rows = e[pl.ds(pl.multiple_of(t * FEAT, FEAT), FEAT), :]
        pe_part[:, :, t] = dot_wide2(qt[...], rows, NT).reshape(2, NX, 8, FEAT)
        return carry

    lax.fori_loop(0, NZ, error_rows, 0)
    swap(0, pe_part.at[o], pe_c)

    finish("z", 0, lambda i: h_rs.at[i])
    h_ag[z] = jnp.sum(h_rs[...].astype(F32), axis=0).astype(BF16)
    start("z", 1, lambda j: h_ag.at[z], lambda i: h_ag.at[i])

    product(shifted(0, 2))
    product(shifted(1, 2))
    swapped(0, pe_c)
    pe_c[...] += pe_part[c]
    start("x", 0, lambda j: pe_c.at[j], lambda i: pe_x.at[i])
    pe_x[x] = pe_c[x]
    product(shifted(0, 1))
    product(shifted(1, 1))
    product(z)
    pump(2)

    loads[5].wait()
    finish("z", 1, lambda i: h_ag.at[i])
    h_all = unpair_rows(h_ag[...].astype(F32)).reshape(R, TOK).astype(BF16)
    px_part[...] = dot(h_all, xt[...], NT).reshape(2, NX, 8, FEAT)
    swap(1, px_part.at[o], px_c)

    finish("x", 0, lambda i: pe_x.at[i])
    pe_x[x] = pe_x[0] + pe_x[1] + pe_x[2] + pe_x[3]
    start("z", 2, lambda j: pe_x.at[x, j], lambda i: pe_z.at[i])
    pe_z[z] = pe_x[x, z]

    swapped(1, px_c)
    px_c[...] += px_part[c]
    start("x", 1, lambda j: px_c.at[j], lambda i: px_x.at[i])
    px_x[x] = px_c[x]
    pump(1)
    finish("x", 1, lambda i: px_x.at[i])
    finish("z", 2, lambda i: pe_z.at[i])
    px_y[y] = jnp.sum(px_x[...], axis=0) + jnp.sum(pe_z[...], axis=0)
    start("y", 0, lambda j: px_y.at[y], lambda i: px_y.at[i])
    pump(1)
    finish("y", 0, lambda i: px_y.at[i])
    p_row = jnp.sum(px_y[...], axis=0)
    pt[c, x] = p_row
    pf[c, x, z] = p_row
    start("x", 2, lambda j: pt.at[c, x], lambda i: pt.at[c, i])
    start("z", 3, lambda j: pf.at[c, x, z], lambda i: pf.at[c, x, i])
    pump(1)
    finish("x", 2, lambda i: pt.at[c, i])
    swap(2, pt.at[c], pt.at[c])
    swapped(2, pt.at[o])

    z_sum = dot_wide(pt[...].reshape(R, FEAT), xt[...], NN).reshape(NZ, 8, TOK)
    z_part[...] = pair_rows(z_sum).astype(BF16)
    start("z", 4, lambda j: z_part.at[j], lambda i: z_rs.at[i])
    z_rs[z] = z_part[z]

    finish("z", 3, lambda i: pf.at[c, x, i])
    start("x", 3, lambda j: pf.at[c, x], lambda i: pf.at[c, i])
    pump(2)

    finish("z", 4, lambda i: z_rs.at[i])
    z_ag[z] = jnp.sum(z_rs[...].astype(F32), axis=0).astype(BF16)
    start("z", 5, lambda j: z_ag.at[z], lambda i: z_ag.at[i])

    finish("x", 3, lambda i: pf.at[c, i])
    swap(3, pf.at[c], pf.at[c])
    pump(1)
    swapped(3, pf.at[o])

    def features(t, gram):
        block = pf[:, :, t].reshape(R, FEAT)
        rows = e[pl.ds(pl.multiple_of(t * FEAT, FEAT), FEAT), :]
        y_err[...] += dot_wide2(block, rows, NN)
        return gram + lax.dot_general(block, block, NT, precision=highest, preferred_element_type=F32)

    y_err[...] = jnp.zeros_like(y_err)
    gram = lax.fori_loop(0, NZ, features, jnp.zeros((R, R), F32))
    eye = (lax.broadcasted_iota(jnp.int32, (R, R), 0) == lax.broadcasted_iota(jnp.int32, (R, R), 1)).astype(F32)
    work[...] = jnp.concatenate([gram, eye], axis=1)

    pump(1)
    finish("z", 5, lambda i: z_ag.at[i])
    z_all = unpair_rows(z_ag[...].astype(F32)).reshape(R, TOK).astype(BF16)
    y_part[...] = (y_err[...] + dot(z_all, g[...], NN)).reshape(2, NX, 8, HID)
    swap(4, y_part.at[o], y_c)
    eliminate(work, 0, 8)
    swapped(4, y_c)
    y_c[...] += y_part[c]
    start("x", 4, lambda j: y_c.at[j], lambda i: y_x.at[i])
    y_x[x] = y_c[x]
    pump(1)
    eliminate(work, 8, 24)
    finish("x", 4, lambda i: y_x.at[i])
    y_y[y] = jnp.sum(y_x[...], axis=0)
    start("y", 1, lambda j: y_y.at[y], lambda i: y_y.at[i])
    pump(1)
    eliminate(work, 24, 40)
    finish("y", 1, lambda i: y_y.at[i])
    y_f[c, x] = jnp.sum(y_y[...], axis=0)
    start("x", 5, lambda j: y_f.at[c, x], lambda i: y_f.at[c, i])
    pump(1)
    eliminate(work, 40, 56)
    finish("x", 5, lambda i: y_f.at[c, i])
    swap(5, y_f.at[c], y_f.at[c])
    eliminate(work, 56, 64)
    diag = jnp.sum(work[:, :R] * eye, axis=1, keepdims=True)
    inverse = work[:, R:] * (lax.rsqrt(diag) * (1.0 / (NX * NY * 2)))
    pump(len(events))
    for half in range(2):
        for ch in range(NCH):
            rows = pl.ds(half * HALF + ch * CHUNK, CHUNK)
            long, short = ring[half, 6, ch].astype(F32), ring[1 - half, 5, ch].astype(F32)
            gi_out[rows, :] = (part[z, rows].astype(F32) + long + short).astype(BF16)
    swapped(5, y_f.at[o])
    q_out[...] = lax.dot_general(
        inverse, y_f[...].reshape(R, HID), NN, precision=highest, preferred_element_type=F32)
    for cp in sent:
        cp.wait_send()


def local(tokens, w_in, pre_act, grad_hidden, err_state, q_init):
    vm = lambda *shape: pltpu.VMEM(shape, F32)
    vb = lambda *shape: pltpu.VMEM(shape, BF16)
    dma = pltpu.SemaphoreType.DMA
    q_factor, grad_input = pl.pallas_call(
        kernel,
        out_shape=[jax.ShapeDtypeStruct((R, HID), F32), jax.ShapeDtypeStruct((FEAT, TOK), BF16)],
        in_specs=[pl.BlockSpec(memory_space=pl.ANY)] * 6,
        out_specs=[pl.BlockSpec(memory_space=pltpu.VMEM)] * 2,
        scratch_shapes=[vb(TOK, HID), vb(TOK, HID), vm(R, HID), vb(NZ * FEAT, HID), vm(NZ * FEAT, HID),
                        vb(FEAT, TOK), vb(TOK, HID), vb(NZ, FEAT, TOK), vb(2, 7, NCH, CHUNK, TOK)]
        + [vb(NZ, 16, TOK // 2)] * 6
        + [vm(2, NX, 8, FEAT), vm(NX, 8, FEAT), vm(NX, 8, FEAT), vm(NY, 8, FEAT), vm(2, NX, 8, FEAT)]
        + [vm(2, NX, NZ, 8, FEAT), vm(NX, NZ, 8, FEAT), vm(NX, NZ, 8, FEAT), vm(NZ, 8, FEAT), vm(2, NX, NZ, 8, FEAT)]
        + [vm(2, NX, 8, HID), vm(NX, 8, HID), vm(NX, 8, HID), vm(NY, 8, HID), vm(2, NX, 8, HID), vm(R, HID),
           vm(R, 2 * R)]
        + [dma((6, NZ)), dma((6, NZ)), dma((6, NX)), dma((6, NX)), dma((2, NY)), dma((2, NY)), dma((6,)), dma((6,)),
           dma((2, 7, NCH)), dma((2, 7, NCH)), dma((6,))],
        compiler_params=pltpu.CompilerParams(
            collective_id=0, has_side_effects=True, vmem_limit_bytes=56 << 20),
        name="backward",
    )(pre_act, grad_hidden, q_init.T, w_in, err_state[0], tokens.T)
    return (grad_input.T, q_factor.T)


def solution(mesh):
    return jax.shard_map(
        local,
        mesh=mesh,
        in_specs=(
            P("dp", "tensor"),
            P(None, "tensor"),
            P("dp", "tensor"),
            P("dp", "tensor"),
            P("dp", None, "tensor"),
            P("tensor", None),
        ),
        out_specs=(P("dp", "tensor"), P("tensor", None)),
        check_vma=False,
    )
```

time: 120 us -> 79.4 us (0.66)
  between operations: 14.1 us -> 0.64 us
  Pallas kernels: 86.7 us -> 75.1 us
  local copies, waits for them, and re-layouts: 11.1 us -> 3.43 us
  matrix products: 4.81 us -> 0 us
  other arithmetic: 3.02 us -> 0 us
    pallas_call x1, Pallas kernels: 86.7 us -> 75.1 us  [local(): pl.pallas_call(kernel, out_shape=[jax.ShapeDtypeStruct((R, HID), F32), ja...]
    unnamed x12 -> x2, local copies, waits for them, and re-layouts: 11.1 us -> 3.43 us
    dot_general x1 -> x0, matrix products: 4.81 us -> none  [dot(): return lax.dot_general(left, right, dims, preferred_element_type=F32)]
    convert_element_type x1 -> x0, other arithmetic: 3.02 us -> none  [local(): pre_grad = (grad_hidden.astype(F32) * slopes).astype(BF16)]
  transfers between devices with their start and end apart: 1 -> 0, of which waited for: 0 -> 0; matrix products, arithmetic and copies ran while one was open for 0% -> 0% of each run, Pallas kernels for 72% -> 0%
where the time goes in v2:
time: 79.4 us; the launch traced here: 79.2 us
  Pallas kernels  75.1 us (95%)
  local copies, waits for them, and re-layouts  3.43 us (4%)
    pallas_call x1, Pallas kernels, local(): pl.pallas_call(kernel, out_shape=[jax.ShapeDtypeStruct((R, HID), F32), ja...  75.1 us
    unnamed x2, local copies, waits for them, and re-layouts  3.43 us

profile of v2, /device:TPU:1, one launch (start us, length us, event | category | flops | bytes accessed | tf_op | source)
XLA Modules:
  0.0 79.2 jit_solution(12981722828346341139)
XLA Ops:
  0.6 75.1 %backward.1 = (f32[64,640]{1,0:T(8,128)}, bf16[320,768]{1,0:T(8,128)(2,1)}) custom-call(bf16[768,640]{1,0:T(8,128)(2,1)} %pre_hbm.1, bf16[768,640]{1,0:T(8,128)(2,1)} %gh_hbm.1, f32[64,640]{1,0:T(8,128)} %bitcast.9, bf16[2560,640]{1,0:T(8,128)(2,1)} %w_hbm.1, f32[2560,640]{1,0:T(8,128)} %bitcast.5, bf16[320,768]{1,0:T(8,128)(2,1)} %bitcast.6), custom_call_target="tpu_custom_call" | custom-call | tf_op jit(solution)/shard_map/backward/pallas_call | solution.py:326
  75.8 1.8 %copy.10 = bf16[768,320]{0,1:T(8,128)(2,1)} copy(bf16[768,320]{0,1:T(8,128)(2,1)} %bitcast.7) | data formatting | bytes 983040
  77.6 1.6 %copy.11 = f32[640,64]{0,1:T(8,128)} copy(f32[640,64]{0,1:T(8,128)} %bitcast.8) | data formatting | bytes 327680

commit v3 on v2

--- a/solution.py
+++ b/solution.py
@@ -41,7 +41,7 @@
     return both[:rows] + both[rows:]
 
 
-def dot_wide2(left, right, dims):
+def dot_both(left, right, dims):
     high, low = halves(right)
     return dot_wide(left, high, dims) + dot(left.astype(BF16), low, dims)
 
@@ -68,7 +68,7 @@
 
 def kernel(
     pre_hbm, gh_hbm, qt_hbm, w_hbm, e_hbm, xt_hbm, q_out, gi_out,
-    pre, gh, qt, w, e, xt, g, part, ring,
+    pre, gh, qt, w, e, xt, g, eb, part, ring,
     h_part, h_rs, h_ag, z_part, z_rs, z_ag,
     px_part, px_c, px_x, px_y, pt,
     pe_part, pe_c, pe_x, pe_z, pf,
@@ -155,19 +155,24 @@
         rows = w[pl.ds(pl.multiple_of(t * FEAT, FEAT), FEAT), :]
         part[t] = dot(rows, g[...], NT).astype(BF16)
 
-    loads = [
-        pltpu.make_async_copy(src, dst, s_in.at[i])
-        for i, (src, dst) in enumerate(
-            [(pre_hbm, pre), (gh_hbm, gh), (qt_hbm, qt), (w_hbm, w), (e_hbm, e), (xt_hbm, xt)])
-    ]
-    for cp in loads:
-        cp.start()
+    def drain():
+        while sent:
+            sent.pop(0).wait_send()
+
     barrier = pltpu.get_barrier_semaphore()
-    for axis in "zxy":
+    for axis in "zyx":
         n, me, dev = axes[axis][:3]
         for k in range(1, n):
             pl.semaphore_signal(barrier, inc=1, device_id=dev(lax.rem(me + k, n)), device_id_type=MESH)
     pl.semaphore_signal(barrier, inc=1, device_id=at(y, x, o, z), device_id_type=MESH)
+    loads = [
+        pltpu.make_async_copy(src, dst, s_in.at[i])
+        for i, (src, dst) in enumerate(
+            [(pre_hbm, pre), (gh_hbm, gh), (qt_hbm, qt), (e_hbm, e), (w_hbm, w), (xt_hbm, xt)])
+    ]
+    for cp in loads:
+        cp.start()
+    eye = (lax.broadcasted_iota(jnp.int32, (R, R), 0) == lax.broadcasted_iota(jnp.int32, (R, R), 1)).astype(F32)
 
     loads[0].wait()
     loads[1].wait()
@@ -180,11 +185,20 @@
     lax.fori_loop(0, TOK // 64, activate, 0)
     loads[2].wait()
     h_part[...] = pair_rows(dot_wide(qt[...], g[...], NT).reshape(NZ, 8, TOK)).astype(BF16)
+    loads[3].wait()
+
+    def error_rows(t, carry):
+        rows = pl.ds(pl.multiple_of(t * FEAT, FEAT), FEAT)
+        eb[rows, :] = e[rows, :].astype(BF16)
+        pe_part[:, :, t] = dot_wide(qt[...], eb[rows, :], NT).reshape(2, NX, 8, FEAT)
+        return carry
+
+    lax.fori_loop(0, NZ, error_rows, 0)
     pl.semaphore_wait(barrier, 14)
     start("z", 0, lambda j: h_part.at[j], lambda i: h_rs.at[i])
+    swap(0, pe_part.at[o], pe_c)
     h_rs[z] = h_part[z]
-
-    loads[3].wait()
+    loads[4].wait()
     product(shifted(0, 4))
     ring_first(0, 0)
     ring_first(1, 0)
@@ -192,51 +206,37 @@
     ring_first(0, 1)
     product(shifted(1, 3))
     ring_first(1, 1)
-
-    loads[4].wait()
-
-    def error_rows(t, carry):
-        rows = e[pl.ds(pl.multiple_of(t * FEAT, FEAT), FEAT), :]
-        pe_part[:, :, t] = dot_wide2(qt[...], rows, NT).reshape(2, NX, 8, FEAT)
-        return carry
-
-    lax.fori_loop(0, NZ, error_rows, 0)
-    swap(0, pe_part.at[o], pe_c)
-
-    finish("z", 0, lambda i: h_rs.at[i])
-    h_ag[z] = jnp.sum(h_rs[...].astype(F32), axis=0).astype(BF16)
-    start("z", 1, lambda j: h_ag.at[z], lambda i: h_ag.at[i])
-
-    product(shifted(0, 2))
-    product(shifted(1, 2))
     swapped(0, pe_c)
     pe_c[...] += pe_part[c]
     start("x", 0, lambda j: pe_c.at[j], lambda i: pe_x.at[i])
     pe_x[x] = pe_c[x]
+    product(shifted(0, 2))
+    finish("z", 0, lambda i: h_rs.at[i])
+    h_ag[z] = jnp.sum(h_rs[...].astype(F32), axis=0).astype(BF16)
+    start("z", 1, lambda j: h_ag.at[z], lambda i: h_ag.at[i])
+    product(shifted(1, 2))
     product(shifted(0, 1))
     product(shifted(1, 1))
     product(z)
+    finish("x", 0, lambda i: pe_x.at[i])
+    pe_x[x] = pe_x[0] + pe_x[1] + pe_x[2] + pe_x[3]
+    start("z", 2, lambda j: pe_x.at[x, j], lambda i: pe_z.at[i])
+    pe_z[z] = pe_x[x, z]
+    loads[5].wait()
     pump(2)
-
-    loads[5].wait()
     finish("z", 1, lambda i: h_ag.at[i])
     h_all = unpair_rows(h_ag[...].astype(F32)).reshape(R, TOK).astype(BF16)
     px_part[...] = dot(h_all, xt[...], NT).reshape(2, NX, 8, FEAT)
     swap(1, px_part.at[o], px_c)
-
-    finish("x", 0, lambda i: pe_x.at[i])
-    pe_x[x] = pe_x[0] + pe_x[1] + pe_x[2] + pe_x[3]
-    start("z", 2, lambda j: pe_x.at[x, j], lambda i: pe_z.at[i])
-    pe_z[z] = pe_x[x, z]
-
     swapped(1, px_c)
     px_c[...] += px_part[c]
     start("x", 1, lambda j: px_c.at[j], lambda i: px_x.at[i])
     px_x[x] = px_c[x]
     pump(1)
+    finish("z", 2, lambda i: pe_z.at[i])
+    pe_sum = jnp.sum(pe_z[...], axis=0)
     finish("x", 1, lambda i: px_x.at[i])
-    finish("z", 2, lambda i: pe_z.at[i])
-    px_y[y] = jnp.sum(px_x[...], axis=0) + jnp.sum(pe_z[...], axis=0)
+    px_y[y] = jnp.sum(px_x[...], axis=0) + pe_sum
     start("y", 0, lambda j: px_y.at[y], lambda i: px_y.at[i])
     pump(1)
     finish("y", 0, lambda i: px_y.at[i])
@@ -249,20 +249,16 @@
     finish("x", 2, lambda i: pt.at[c, i])
     swap(2, pt.at[c], pt.at[c])
     swapped(2, pt.at[o])
-
     z_sum = dot_wide(pt[...].reshape(R, FEAT), xt[...], NN).reshape(NZ, 8, TOK)
     z_part[...] = pair_rows(z_sum).astype(BF16)
     start("z", 4, lambda j: z_part.at[j], lambda i: z_rs.at[i])
     z_rs[z] = z_part[z]
-
     finish("z", 3, lambda i: pf.at[c, x, i])
     start("x", 3, lambda j: pf.at[c, x], lambda i: pf.at[c, i])
     pump(2)
-
     finish("z", 4, lambda i: z_rs.at[i])
     z_ag[z] = jnp.sum(z_rs[...].astype(F32), axis=0).astype(BF16)
     start("z", 5, lambda j: z_ag.at[z], lambda i: z_ag.at[i])
-
     finish("x", 3, lambda i: pf.at[c, i])
     swap(3, pf.at[c], pf.at[c])
     pump(1)
@@ -270,16 +266,15 @@
 
     def features(t, gram):
         block = pf[:, :, t].reshape(R, FEAT)
-        rows = e[pl.ds(pl.multiple_of(t * FEAT, FEAT), FEAT), :]
-        y_err[...] += dot_wide2(block, rows, NN)
+        rows = pl.ds(pl.multiple_of(t * FEAT, FEAT), FEAT)
+        y_err[...] += dot_wide(block, eb[rows, :], NN)
         return gram + lax.dot_general(block, block, NT, precision=highest, preferred_element_type=F32)
 
     y_err[...] = jnp.zeros_like(y_err)
     gram = lax.fori_loop(0, NZ, features, jnp.zeros((R, R), F32))
-    eye = (lax.broadcasted_iota(jnp.int32, (R, R), 0) == lax.broadcasted_iota(jnp.int32, (R, R), 1)).astype(F32)
     work[...] = jnp.concatenate([gram, eye], axis=1)
-
-    pump(1)
+    pump(1)
+    drain()
     finish("z", 5, lambda i: z_ag.at[i])
     z_all = unpair_rows(z_ag[...].astype(F32)).reshape(R, TOK).astype(BF16)
     y_part[...] = (y_err[...] + dot(z_all, g[...], NN)).reshape(2, NX, 8, HID)
@@ -313,10 +308,16 @@
             long, short = ring[half, 6, ch].astype(F32), ring[1 - half, 5, ch].astype(F32)
             gi_out[rows, :] = (part[z, rows].astype(F32) + long + short).astype(BF16)
     swapped(5, y_f.at[o])
-    q_out[...] = lax.dot_general(
-        inverse, y_f[...].reshape(R, HID), NN, precision=highest, preferred_element_type=F32)
-    for cp in sent:
-        cp.wait_send()
+    q_out[...] = dot_both(inverse, y_f[...].reshape(R, HID), NN)
+    drain()
+
+
+def deliver(q_ref, gi_ref, q_out, gi_out, sems):
+    copies = [pltpu.make_async_copy(q_ref, q_out, sems.at[0]), pltpu.make_async_copy(gi_ref, gi_out, sems.at[1])]
+    for cp in copies:
+        cp.start()
+    for cp in copies:
+        cp.wait()
 
 
 def local(tokens, w_in, pre_act, grad_hidden, err_state, q_init):
@@ -329,7 +330,7 @@
         in_specs=[pl.BlockSpec(memory_space=pl.ANY)] * 6,
         out_specs=[pl.BlockSpec(memory_space=pltpu.VMEM)] * 2,
         scratch_shapes=[vb(TOK, HID), vb(TOK, HID), vm(R, HID), vb(NZ * FEAT, HID), vm(NZ * FEAT, HID),
-                        vb(FEAT, TOK), vb(TOK, HID), vb(NZ, FEAT, TOK), vb(2, 7, NCH, CHUNK, TOK)]
+                        vb(FEAT, TOK), vb(TOK, HID), vb(NZ * FEAT, HID), vb(NZ, FEAT, TOK), vb(2, 7, NCH, CHUNK, TOK)]
         + [vb(NZ, 16, TOK // 2)] * 6
         + [vm(2, NX, 8, FEAT), vm(NX, 8, FEAT), vm(NX, 8, FEAT), vm(NY, 8, FEAT), vm(2, NX, 8, FEAT)]
         + [vm(2, NX, NZ, 8, FEAT), vm(NX, NZ, 8, FEAT), vm(NX, NZ, 8, FEAT), vm(NZ, 8, FEAT), vm(2, NX, NZ, 8, FEAT)]
@@ -341,6 +342,15 @@
             collective_id=0, has_side_effects=True, vmem_limit_bytes=56 << 20),
         name="backward",
     )(pre_act, grad_hidden, q_init.T, w_in, err_state[0], tokens.T)
+    q_factor, grad_input = pl.pallas_call(
+        deliver,
+        out_shape=[jax.ShapeDtypeStruct((R, HID), F32), jax.ShapeDtypeStruct((FEAT, TOK), BF16)],
+        in_specs=[pl.BlockSpec(memory_space=pl.ANY)] * 2,
+        out_specs=[pl.BlockSpec(memory_space=pl.ANY)] * 2,
+        scratch_shapes=[dma((2,))],
+        compiler_params=pltpu.CompilerParams(vmem_limit_bytes=56 << 20),
+        name="deliver",
+    )(q_factor, grad_input)
     return (grad_input.T, q_factor.T)
 
 

time: 79.4 us -> 99.7 us (1.26)
  Pallas kernels: 75.1 us -> 99 us
  local copies, waits for them, and re-layouts: 3.43 us -> 0 us
    pallas_call x0 -> x1, Pallas kernels: none -> 21 us  [local(): pl.pallas_call(deliver, out_shape=[jax.ShapeDtypeStruct((R, HID), F32), j...]
    unnamed x2 -> x0, local copies, waits for them, and re-layouts: 3.43 us -> none
    pallas_call x1, Pallas kernels: 75.1 us -> 78 us  [local(): pl.pallas_call(kernel, out_shape=[jax.ShapeDtypeStruct((R, HID), F32), ja...]
where the time goes in v3:
time: 99.7 us; the launch traced here: 99.6 us
  Pallas kernels  99 us (99%)
    pallas_call x1, Pallas kernels, local(): pl.pallas_call(kernel, out_shape=[jax.ShapeDtypeStruct((R, HID), F32), ja...  78 us
    pallas_call x1, Pallas kernels, local(): pl.pallas_call(deliver, out_shape=[jax.ShapeDtypeStruct((R, HID), F32), j...  21 us

profile of v3, /device:TPU:1, one launch (start us, length us, event | category | flops | bytes accessed | tf_op | source)
XLA Modules:
  0.0 99.6 jit_solution(9526680102854418039)
XLA Ops:
  0.6 78.0 %backward.1 = (f32[64,640]{1,0:T(8,128)}, bf16[320,768]{1,0:T(8,128)(2,1)}) custom-call(bf16[768,640]{1,0:T(8,128)(2,1)} %pre_hbm.1, bf16[768,640]{1,0:T(8,128)(2,1)} %gh_hbm.1, f32[64,640]{1,0:T(8,128)} %bitcast.7, bf16[2560,640]{1,0:T(8,128)(2,1)} %w_hbm.1, f32[2560,640]{1,0:T(8,128)} %bitcast.5, bf16[320,768]{1,0:T(8,128)(2,1)} %bitcast.6), custom_call_target="tpu_custom_call" | custom-call | tf_op jit(solution)/shard_map/backward/pallas_call | solution.py:327
  78.6 21.0 %deliver.1 = (f32[64,640]{1,0:T(8,128)}, bf16[320,768]{1,0:T(8,128)(2,1)}) custom-call(f32[64,640]{1,0:T(8,128)} %get-tuple-element.6.q_ref, bf16[320,768]{1,0:T(8,128)(2,1)} %get-tuple-element.7.gi_ref), custom_call_target="tpu_custom_call" | custom-call | tf_op jit(solution)/shard_map/deliver/pallas_call | solution.py:345

commit v4 on v3

--- a/solution.py
+++ b/solution.py
@@ -55,15 +55,17 @@
     return jnp.concatenate([value[..., :8, :], value[..., 8:, :]], axis=-1)
 
 
-def eliminate(work, first, last):
-    whole = work[...]
-    below = lax.broadcasted_iota(jnp.int32, (R, 1), 0)
-    for k in range(first, last):
-        row = whole[k:k + 1, :]
-        column = whole[:, k:k + 1]
-        ratio = jnp.where(below > k, column / whole[k:k + 1, k:k + 1], 0.0)
-        whole = whole - ratio * row
-    work[...] = whole
+def eliminate(work, first, last, here):
+    @pl.when(here)
+    def _():
+        whole = work[...]
+        below = lax.broadcasted_iota(jnp.int32, (R, 1), 0)
+        for k in range(first, last):
+            row = whole[k:k + 1, :]
+            column = whole[:, k:k + 1]
+            ratio = jnp.where(below > k, column / whole[k:k + 1, k:k + 1], 0.0)
+            whole = whole - ratio * row
+        work[...] = whole
 
 
 def kernel(
@@ -159,71 +161,90 @@
         while sent:
             sent.pop(0).wait_send()
 
+    def load(src, dst, i):
+        cp = pltpu.make_async_copy(src, dst, s_in.at[i])
+        cp.start()
+        return cp
+
+    def block(t):
+        return pl.ds(pl.multiple_of(t * FEAT, FEAT), FEAT)
+
+    order = [shifted(0, 4), shifted(0, 3), shifted(1, 3), shifted(0, 2), shifted(1, 2), shifted(0, 1), shifted(1, 1), z]
+
+    def load_w(i):
+        return load(w_hbm.at[block(order[i])], w.at[block(order[i])], 4 + i)
+
+    def load_e(t):
+        return pltpu.make_async_copy(e_hbm.at[block(t)], e.at[block(t)], s_in.at[12 + t])
+
+    loads = [load(pre_hbm, pre, 0), load(gh_hbm, gh, 1), load(qt_hbm, qt, 2)]
     barrier = pltpu.get_barrier_semaphore()
     for axis in "zyx":
         n, me, dev = axes[axis][:3]
         for k in range(1, n):
             pl.semaphore_signal(barrier, inc=1, device_id=dev(lax.rem(me + k, n)), device_id_type=MESH)
     pl.semaphore_signal(barrier, inc=1, device_id=at(y, x, o, z), device_id_type=MESH)
-    loads = [
-        pltpu.make_async_copy(src, dst, s_in.at[i])
-        for i, (src, dst) in enumerate(
-            [(pre_hbm, pre), (gh_hbm, gh), (qt_hbm, qt), (e_hbm, e), (w_hbm, w), (xt_hbm, xt)])
-    ]
-    for cp in loads:
-        cp.start()
     eye = (lax.broadcasted_iota(jnp.int32, (R, R), 0) == lax.broadcasted_iota(jnp.int32, (R, R), 1)).astype(F32)
 
     loads[0].wait()
     loads[1].wait()
+    w_loads = [load_w(i) for i in range(3)]
+    for t in range(NZ):
+        load_e(t).start()
+    w_loads += [load_w(i) for i in range(3, NZ)]
+    x_load = load(xt_hbm, xt, 3)
 
     def activate(i, carry):
-        rows = pl.ds(pl.multiple_of(i * 64, 64), 64)
+        rows = pl.ds(pl.multiple_of(i * 32, 32), 32)
         g[rows, :] = (gh[rows, :].astype(F32) * gelu_slope(pre[rows, :].astype(F32))).astype(BF16)
         return carry
 
-    lax.fori_loop(0, TOK // 64, activate, 0)
+    lax.fori_loop(0, TOK // 32, activate, 0)
     loads[2].wait()
     h_part[...] = pair_rows(dot_wide(qt[...], g[...], NT).reshape(NZ, 8, TOK)).astype(BF16)
-    loads[3].wait()
-
-    def error_rows(t, carry):
-        rows = pl.ds(pl.multiple_of(t * FEAT, FEAT), FEAT)
-        eb[rows, :] = e[rows, :].astype(BF16)
-        pe_part[:, :, t] = dot_wide(qt[...], eb[rows, :], NT).reshape(2, NX, 8, FEAT)
-        return carry
-
-    lax.fori_loop(0, NZ, error_rows, 0)
     pl.semaphore_wait(barrier, 14)
     start("z", 0, lambda j: h_part.at[j], lambda i: h_rs.at[i])
-    swap(0, pe_part.at[o], pe_c)
     h_rs[z] = h_part[z]
-    loads[4].wait()
-    product(shifted(0, 4))
+    w_loads[0].wait()
+    product(order[0])
     ring_first(0, 0)
     ring_first(1, 0)
-    product(shifted(0, 3))
+
+    def error_rows(t, carry):
+        load_e(t).wait()
+        eb[block(t), :] = e[block(t), :].astype(BF16)
+        pe_part[:, :, t] = dot_wide(qt[...], eb[block(t), :], NT).reshape(2, NX, 8, FEAT)
+        return carry
+
+    lax.fori_loop(0, NZ, error_rows, 0)
+    swap(0, pe_part.at[o], pe_c)
+    w_loads[1].wait()
+    product(order[1])
     ring_first(0, 1)
-    product(shifted(1, 3))
+    w_loads[2].wait()
+    product(order[2])
     ring_first(1, 1)
     swapped(0, pe_c)
     pe_c[...] += pe_part[c]
     start("x", 0, lambda j: pe_c.at[j], lambda i: pe_x.at[i])
     pe_x[x] = pe_c[x]
-    product(shifted(0, 2))
     finish("z", 0, lambda i: h_rs.at[i])
     h_ag[z] = jnp.sum(h_rs[...].astype(F32), axis=0).astype(BF16)
     start("z", 1, lambda j: h_ag.at[z], lambda i: h_ag.at[i])
-    product(shifted(1, 2))
-    product(shifted(0, 1))
-    product(shifted(1, 1))
-    product(z)
+    for cp in w_loads[3:]:
+        cp.wait()
+
+    def products(k, carry):
+        product(lax.rem(z + NZ - 2 + k, NZ))
+        return carry
+
+    lax.fori_loop(0, 5, products, 0)
     finish("x", 0, lambda i: pe_x.at[i])
     pe_x[x] = pe_x[0] + pe_x[1] + pe_x[2] + pe_x[3]
     start("z", 2, lambda j: pe_x.at[x, j], lambda i: pe_z.at[i])
     pe_z[z] = pe_x[x, z]
-    loads[5].wait()
-    pump(2)
+    x_load.wait()
+    pump(1)
     finish("z", 1, lambda i: h_ag.at[i])
     h_all = unpair_rows(h_ag[...].astype(F32)).reshape(R, TOK).astype(BF16)
     px_part[...] = dot(h_all, xt[...], NT).reshape(2, NX, 8, FEAT)
@@ -232,7 +253,7 @@
     px_c[...] += px_part[c]
     start("x", 1, lambda j: px_c.at[j], lambda i: px_x.at[i])
     px_x[x] = px_c[x]
-    pump(1)
+    pump(2)
     finish("z", 2, lambda i: pe_z.at[i])
     pe_sum = jnp.sum(pe_z[...], axis=0)
     finish("x", 1, lambda i: px_x.at[i])
@@ -265,10 +286,9 @@
     swapped(3, pf.at[o])
 
     def features(t, gram):
-        block = pf[:, :, t].reshape(R, FEAT)
-        rows = pl.ds(pl.multiple_of(t * FEAT, FEAT), FEAT)
-        y_err[...] += dot_wide(block, eb[rows, :], NN)
-        return gram + lax.dot_general(block, block, NT, precision=highest, preferred_element_type=F32)
+        rows = pf[:, :, t].reshape(R, FEAT)
+        y_err[...] += dot_wide(rows, eb[block(t), :], NN)
+        return gram + lax.dot_general(rows, rows, NT, precision=highest, preferred_element_type=F32)
 
     y_err[...] = jnp.zeros_like(y_err)
     gram = lax.fori_loop(0, NZ, features, jnp.zeros((R, R), F32))
@@ -279,26 +299,26 @@
     z_all = unpair_rows(z_ag[...].astype(F32)).reshape(R, TOK).astype(BF16)
     y_part[...] = (y_err[...] + dot(z_all, g[...], NN)).reshape(2, NX, 8, HID)
     swap(4, y_part.at[o], y_c)
-    eliminate(work, 0, 8)
+    eliminate(work, 0, 8, z >= 0)
     swapped(4, y_c)
     y_c[...] += y_part[c]
     start("x", 4, lambda j: y_c.at[j], lambda i: y_x.at[i])
     y_x[x] = y_c[x]
     pump(1)
-    eliminate(work, 8, 24)
+    eliminate(work, 8, 24, z >= 0)
     finish("x", 4, lambda i: y_x.at[i])
     y_y[y] = jnp.sum(y_x[...], axis=0)
     start("y", 1, lambda j: y_y.at[y], lambda i: y_y.at[i])
     pump(1)
-    eliminate(work, 24, 40)
+    eliminate(work, 24, 40, z >= 0)
     finish("y", 1, lambda i: y_y.at[i])
     y_f[c, x] = jnp.sum(y_y[...], axis=0)
     start("x", 5, lambda j: y_f.at[c, x], lambda i: y_f.at[c, i])
     pump(1)
-    eliminate(work, 40, 56)
+    eliminate(work, 40, 56, z >= 0)
     finish("x", 5, lambda i: y_f.at[c, i])
     swap(5, y_f.at[c], y_f.at[c])
-    eliminate(work, 56, 64)
+    eliminate(work, 56, 64, z >= 0)
     diag = jnp.sum(work[:, :R] * eye, axis=1, keepdims=True)
     inverse = work[:, R:] * (lax.rsqrt(diag) * (1.0 / (NX * NY * 2)))
     pump(len(events))
@@ -312,12 +332,9 @@
     drain()
 
 
-def deliver(q_ref, gi_ref, q_out, gi_out, sems):
-    copies = [pltpu.make_async_copy(q_ref, q_out, sems.at[0]), pltpu.make_async_copy(gi_ref, gi_out, sems.at[1])]
-    for cp in copies:
-        cp.start()
-    for cp in copies:
-        cp.wait()
+def deliver(q_ref, gi_ref, q_out, gi_out):
+    q_out[...] = q_ref[...]
+    gi_out[...] = gi_ref[...]
 
 
 def local(tokens, w_in, pre_act, grad_hidden, err_state, q_init):
@@ -337,7 +354,7 @@
         + [vm(2, NX, 8, HID), vm(NX, 8, HID), vm(NX, 8, HID), vm(NY, 8, HID), vm(2, NX, 8, HID), vm(R, HID),
            vm(R, 2 * R)]
         + [dma((6, NZ)), dma((6, NZ)), dma((6, NX)), dma((6, NX)), dma((2, NY)), dma((2, NY)), dma((6,)), dma((6,)),
-           dma((2, 7, NCH)), dma((2, 7, NCH)), dma((6,))],
+           dma((2, 7, NCH)), dma((2, 7, NCH)), dma((20,))],
         compiler_params=pltpu.CompilerParams(
             collective_id=0, has_side_effects=True, vmem_limit_bytes=56 << 20),
         name="backward",
@@ -345,9 +362,8 @@
     q_factor, grad_input = pl.pallas_call(
         deliver,
         out_shape=[jax.ShapeDtypeStruct((R, HID), F32), jax.ShapeDtypeStruct((FEAT, TOK), BF16)],
-        in_specs=[pl.BlockSpec(memory_space=pl.ANY)] * 2,
-        out_specs=[pl.BlockSpec(memory_space=pl.ANY)] * 2,
-        scratch_shapes=[dma((2,))],
+        in_specs=[pl.BlockSpec(memory_space=pltpu.VMEM)] * 2,
+        out_specs=[pl.BlockSpec(memory_space=pltpu.VMEM)] * 2,
         compiler_params=pltpu.CompilerParams(vmem_limit_bytes=56 << 20),
         name="deliver",
     )(q_factor, grad_input)

time: 99.7 us -> 78.7 us (0.79)
  Pallas kernels: 99 us -> 77.9 us
    pallas_call x1, Pallas kernels: 21 us -> 1.97 us  [local(): pl.pallas_call(deliver, out_shape=[jax.ShapeDtypeStruct((R, HID), F32), j...]
    pallas_call x1, Pallas kernels: 78 us -> 76 us  [local(): pl.pallas_call(kernel, out_shape=[jax.ShapeDtypeStruct((R, HID), F32), ja...]
where the time goes in v4:
time: 78.7 us; the launch traced here: 78.6 us
  Pallas kernels  77.9 us (99%)
    pallas_call x1, Pallas kernels, local(): pl.pallas_call(kernel, out_shape=[jax.ShapeDtypeStruct((R, HID), F32), ja...  76 us
    pallas_call x1, Pallas kernels, local(): pl.pallas_call(deliver, out_shape=[jax.ShapeDtypeStruct((R, HID), F32), j...  1.97 us

profile of v4, /device:TPU:1, one launch (start us, length us, event | category | flops | bytes accessed | tf_op | source)
XLA Modules:
  0.0 78.6 jit_solution(5625362616374110067)
XLA Ops:
  0.6 76.0 %backward.1 = (f32[64,640]{1,0:T(8,128)}, bf16[320,768]{1,0:T(8,128)(2,1)}) custom-call(bf16[768,640]{1,0:T(8,128)(2,1)} %pre_hbm.1, bf16[768,640]{1,0:T(8,128)(2,1)} %gh_hbm.1, f32[64,640]{1,0:T(8,128)} %bitcast.7, bf16[2560,640]{1,0:T(8,128)(2,1)} %w_hbm.1, f32[2560,640]{1,0:T(8,128)} %bitcast.5, bf16[320,768]{1,0:T(8,128)(2,1)} %bitcast.6), custom_call_target="tpu_custom_call" | custom-call | tf_op jit(solution)/shard_map/backward/pallas_call | solution.py:344
  76.6 2.0 %deliver.1 = (f32[64,640]{1,0:T(8,128)}, bf16[320,768]{1,0:T(8,128)(2,1)}) custom-call(f32[64,640]{1,0:T(8,128)} %get-tuple-element.6.q_ref, bf16[320,768]{1,0:T(8,128)(2,1)} %get-tuple-element.7.gi_ref), custom_call_target="tpu_custom_call" | custom-call | tf_op jit(solution)/shard_map/deliver/pallas_call | solution.py:362

commit v5 on v4

--- a/solution.py
+++ b/solution.py
@@ -15,6 +15,7 @@
 HALF = FEAT // 2
 CHUNK = HALF // NCH
 HOPS = (4, 3, 3, 2, 2, 1, 1)
+SENDS = dict(a=2, b=0, c=0, d=1, e=1, f=1, g=1, h=1, i=1, j=0, k=2, l=0, m=1, n=1, o=1, p=1, q=0)
 NN = (((1,), (0,)), ((), ()))
 NT = (((1,), (1,)), ((), ()))
 
@@ -129,29 +130,25 @@
         push(src, ring.at[direction, m, ch], s_g.at[direction, m, ch], r_g.at[direction, m, ch],
              at(y, x, c, shifted(direction, 1)))
 
-    def ring_first(direction, m):
-        for ch in range(NCH):
-            ring_send(direction, m, ch, part.at[shifted(direction, HOPS[m]), piece(direction, m, ch)])
-
     def ring_wait(direction, m, ch):
         slot = ring.at[direction, m, ch]
         remote(slot, slot, s_g.at[direction, m, ch], r_g.at[direction, m, ch],
                at(y, x, c, shifted(direction, 1))).wait_recv()
 
-    def ring_event(m, ch):
-        for direction in range(2):
-            ring_wait(direction, m, ch)
-            if m < 5:
-                own = part[shifted(direction, HOPS[m + 2]), piece(direction, m, ch)]
-                ring[direction, m, ch] = (ring[direction, m, ch].astype(F32) + own.astype(F32)).astype(BF16)
-                ring_send(direction, m + 2, ch, ring.at[direction, m, ch])
-
-    events = [(m, ch) for m in range(7) for ch in range(NCH)]
-
-    def pump(count):
-        for _ in range(count):
-            if events:
-                ring_event(*events.pop(0))
+    todo = [(m, ch) for m in range(7) for ch in range(NCH)]
+
+    def advance(count):
+        for m, ch in todo[:count]:
+            for direction in range(2):
+                mine = part.at[shifted(direction, HOPS[m]), piece(direction, m, ch)]
+                if m < 2:
+                    ring_send(direction, m, ch, mine)
+                else:
+                    ring_wait(direction, m - 2, ch)
+                    slot = ring.at[direction, m - 2, ch]
+                    slot[...] = (slot[...].astype(F32) + mine[...].astype(F32)).astype(BF16)
+                    ring_send(direction, m, ch, slot)
+        del todo[:count]
 
     def product(t):
         rows = w[pl.ds(pl.multiple_of(t * FEAT, FEAT), FEAT), :]
@@ -207,8 +204,7 @@
     h_rs[z] = h_part[z]
     w_loads[0].wait()
     product(order[0])
-    ring_first(0, 0)
-    ring_first(1, 0)
+    advance(SENDS["a"])
 
     def error_rows(t, carry):
         load_e(t).wait()
@@ -220,10 +216,9 @@
     swap(0, pe_part.at[o], pe_c)
     w_loads[1].wait()
     product(order[1])
-    ring_first(0, 1)
     w_loads[2].wait()
     product(order[2])
-    ring_first(1, 1)
+    advance(SENDS["b"])
     swapped(0, pe_c)
     pe_c[...] += pe_part[c]
     start("x", 0, lambda j: pe_c.at[j], lambda i: pe_x.at[i])
@@ -231,6 +226,7 @@
     finish("z", 0, lambda i: h_rs.at[i])
     h_ag[z] = jnp.sum(h_rs[...].astype(F32), axis=0).astype(BF16)
     start("z", 1, lambda j: h_ag.at[z], lambda i: h_ag.at[i])
+    advance(SENDS["c"])
     for cp in w_loads[3:]:
         cp.wait()
 
@@ -244,29 +240,30 @@
     start("z", 2, lambda j: pe_x.at[x, j], lambda i: pe_z.at[i])
     pe_z[z] = pe_x[x, z]
     x_load.wait()
-    pump(1)
+    advance(SENDS["d"])
     finish("z", 1, lambda i: h_ag.at[i])
     h_all = unpair_rows(h_ag[...].astype(F32)).reshape(R, TOK).astype(BF16)
     px_part[...] = dot(h_all, xt[...], NT).reshape(2, NX, 8, FEAT)
     swap(1, px_part.at[o], px_c)
+    advance(SENDS["e"])
     swapped(1, px_c)
     px_c[...] += px_part[c]
     start("x", 1, lambda j: px_c.at[j], lambda i: px_x.at[i])
     px_x[x] = px_c[x]
-    pump(2)
+    advance(SENDS["f"])
     finish("z", 2, lambda i: pe_z.at[i])
     pe_sum = jnp.sum(pe_z[...], axis=0)
     finish("x", 1, lambda i: px_x.at[i])
     px_y[y] = jnp.sum(px_x[...], axis=0) + pe_sum
     start("y", 0, lambda j: px_y.at[y], lambda i: px_y.at[i])
-    pump(1)
+    advance(SENDS["g"])
     finish("y", 0, lambda i: px_y.at[i])
     p_row = jnp.sum(px_y[...], axis=0)
     pt[c, x] = p_row
     pf[c, x, z] = p_row
     start("x", 2, lambda j: pt.at[c, x], lambda i: pt.at[c, i])
     start("z", 3, lambda j: pf.at[c, x, z], lambda i: pf.at[c, x, i])
-    pump(1)
+    advance(SENDS["h"])
     finish("x", 2, lambda i: pt.at[c, i])
     swap(2, pt.at[c], pt.at[c])
     swapped(2, pt.at[o])
@@ -274,15 +271,16 @@
     z_part[...] = pair_rows(z_sum).astype(BF16)
     start("z", 4, lambda j: z_part.at[j], lambda i: z_rs.at[i])
     z_rs[z] = z_part[z]
+    advance(SENDS["i"])
     finish("z", 3, lambda i: pf.at[c, x, i])
     start("x", 3, lambda j: pf.at[c, x], lambda i: pf.at[c, i])
-    pump(2)
+    advance(SENDS["j"])
     finish("z", 4, lambda i: z_rs.at[i])
     z_ag[z] = jnp.sum(z_rs[...].astype(F32), axis=0).astype(BF16)
     start("z", 5, lambda j: z_ag.at[z], lambda i: z_ag.at[i])
+    advance(SENDS["k"])
     finish("x", 3, lambda i: pf.at[c, i])
     swap(3, pf.at[c], pf.at[c])
-    pump(1)
     swapped(3, pf.at[o])
 
     def features(t, gram):
@@ -293,35 +291,41 @@
     y_err[...] = jnp.zeros_like(y_err)
     gram = lax.fori_loop(0, NZ, features, jnp.zeros((R, R), F32))
     work[...] = jnp.concatenate([gram, eye], axis=1)
-    pump(1)
+    advance(SENDS["l"])
     drain()
     finish("z", 5, lambda i: z_ag.at[i])
     z_all = unpair_rows(z_ag[...].astype(F32)).reshape(R, TOK).astype(BF16)
     y_part[...] = (y_err[...] + dot(z_all, g[...], NN)).reshape(2, NX, 8, HID)
     swap(4, y_part.at[o], y_c)
+    advance(SENDS["m"])
     eliminate(work, 0, 8, z >= 0)
     swapped(4, y_c)
     y_c[...] += y_part[c]
     start("x", 4, lambda j: y_c.at[j], lambda i: y_x.at[i])
     y_x[x] = y_c[x]
-    pump(1)
+    advance(SENDS["n"])
     eliminate(work, 8, 24, z >= 0)
     finish("x", 4, lambda i: y_x.at[i])
     y_y[y] = jnp.sum(y_x[...], axis=0)
     start("y", 1, lambda j: y_y.at[y], lambda i: y_y.at[i])
-    pump(1)
+    advance(SENDS["o"])
     eliminate(work, 24, 40, z >= 0)
     finish("y", 1, lambda i: y_y.at[i])
     y_f[c, x] = jnp.sum(y_y[...], axis=0)
     start("x", 5, lambda j: y_f.at[c, x], lambda i: y_f.at[c, i])
-    pump(1)
+    advance(SENDS["p"])
     eliminate(work, 40, 56, z >= 0)
     finish("x", 5, lambda i: y_f.at[c, i])
     swap(5, y_f.at[c], y_f.at[c])
+    advance(SENDS["q"])
     eliminate(work, 56, 64, z >= 0)
     diag = jnp.sum(work[:, :R] * eye, axis=1, keepdims=True)
     inverse = work[:, R:] * (lax.rsqrt(diag) * (1.0 / (NX * NY * 2)))
-    pump(len(events))
+    advance(len(todo))
+    for m in (5, 6):
+        for ch in range(NCH):
+            for direction in range(2):
+                ring_wait(direction, m, ch)
     for half in range(2):
         for ch in range(NCH):
             rows = pl.ds(half * HALF + ch * CHUNK, CHUNK)

time: 78.7 us -> 72.5 us (0.921)
  Pallas kernels: 77.9 us -> 71.7 us
    pallas_call x1, Pallas kernels: 76 us -> 69.8 us  [local(): pl.pallas_call(kernel, out_shape=[jax.ShapeDtypeStruct((R, HID), F32), ja...]
where the time goes in v5:
time: 72.5 us; the launch traced here: 72.4 us
  Pallas kernels  71.7 us (99%)
    pallas_call x1, Pallas kernels, local(): pl.pallas_call(kernel, out_shape=[jax.ShapeDtypeStruct((R, HID), F32), ja...  69.8 us
    pallas_call x1, Pallas kernels, local(): pl.pallas_call(deliver, out_shape=[jax.ShapeDtypeStruct((R, HID), F32), j...  1.97 us

profile of v5, /device:TPU:1, one launch (start us, length us, event | category | flops | bytes accessed | tf_op | source)
XLA Modules:
  0.0 72.4 jit_solution(10524764873556035888)
XLA Ops:
  0.6 69.8 %backward.1 = (f32[64,640]{1,0:T(8,128)}, bf16[320,768]{1,0:T(8,128)(2,1)}) custom-call(bf16[768,640]{1,0:T(8,128)(2,1)} %pre_hbm.1, bf16[768,640]{1,0:T(8,128)(2,1)} %gh_hbm.1, f32[64,640]{1,0:T(8,128)} %bitcast.7, bf16[2560,640]{1,0:T(8,128)(2,1)} %w_hbm.1, f32[2560,640]{1,0:T(8,128)} %bitcast.5, bf16[320,768]{1,0:T(8,128)(2,1)} %bitcast.6), custom_call_target="tpu_custom_call" | custom-call | tf_op jit(solution)/shard_map/backward/pallas_call | solution.py:348
  70.4 2.0 %deliver.1 = (f32[64,640]{1,0:T(8,128)}, bf16[320,768]{1,0:T(8,128)(2,1)}) custom-call(f32[64,640]{1,0:T(8,128)} %get-tuple-element.6.q_ref, bf16[320,768]{1,0:T(8,128)(2,1)} %get-tuple-element.7.gi_ref), custom_call_target="tpu_custom_call" | custom-call | tf_op jit(solution)/shard_map/deliver/pallas_call | solution.py:366

commit v6 on v5

--- a/solution.py
+++ b/solution.py
@@ -5,7 +5,6 @@
 from jax.experimental.pallas import tpu as pltpu
 from jax.sharding import PartitionSpec as P
 
-highest = lax.Precision.HIGHEST
 slope_coeff = 0.7978845608
 MESH = pl.DeviceIdType.MESH
 F32, BF16 = jnp.float32, jnp.bfloat16
@@ -15,7 +14,8 @@
 HALF = FEAT // 2
 CHUNK = HALF // NCH
 HOPS = (4, 3, 3, 2, 2, 1, 1)
-SENDS = dict(a=2, b=0, c=0, d=1, e=1, f=1, g=1, h=1, i=1, j=0, k=2, l=0, m=1, n=1, o=1, p=1, q=0)
+SENDS = dict(a=2, b=0, c=0, d=1, e=1, f=1, g=1, h=1, i=1, j=0, k=1, l=0, m=2, n=1, o=1, p=1, q=0)
+FAR = {4: (2, 1, 3), 8: (4, 3, 5, 2, 6, 1, 7)}
 NN = (((1,), (0,)), ((), ()))
 NT = (((1,), (1,)), ((), ()))
 
@@ -73,14 +73,14 @@
     pre_hbm, gh_hbm, qt_hbm, w_hbm, e_hbm, xt_hbm, q_out, gi_out,
     pre, gh, qt, w, e, xt, g, eb, part, ring,
     h_part, h_rs, h_ag, z_part, z_rs, z_ag,
-    px_part, px_c, px_x, px_y, pt,
-    pe_part, pe_c, pe_x, pe_z, pf,
+    px_part, px_rs, px_y, pt,
+    pe_part, pe_send, pe_c, pe_x, pe_s, pe_z, pf_row, pf, p_wide,
     y_part, y_c, y_x, y_y, y_f, y_err, work,
-    s_z, r_z, s_x, r_x, s_y, r_y, s_c, r_c, s_g, r_g, s_in,
+    s_z, r_z, s_q, r_q, s_x, r_x, s_y, r_y, s_c, r_c, s_g, r_g, s_in,
 ):
     dp, z = lax.axis_index("dp"), lax.axis_index("tensor")
     c, x, y = lax.rem(dp, 2), lax.rem(dp // 2, NX), dp // (2 * NX)
-    o = 1 - c
+    o, me = 1 - c, c * NX + x
 
     def at(yy, xx, cc, zz):
         return ((yy * NX + xx) * 2 + cc, zz)
@@ -88,6 +88,7 @@
     axes = {
         "z": (NZ, z, lambda j: at(y, x, c, j), s_z, r_z),
         "x": (NX, x, lambda j: at(y, j, c, z), s_x, r_x),
+        "q": (2 * NX, c * NX + x, lambda j: at(y, lax.rem(j, NX), j // NX, z), s_q, r_q),
         "y": (NY, y, lambda j: at(j, x, c, z), s_y, r_y),
     }
     sent = []
@@ -102,15 +103,15 @@
         sent.append(cp)
 
     def start(axis, phase, src, dst):
-        n, me, dev, ss, rs = axes[axis]
-        for k in range(1, n):
-            j = lax.rem(me + k, n)
-            push(src(j), dst(me), ss.at[phase, k], rs.at[phase, me], dev(j))
+        n, own, dev, ss, rs = axes[axis]
+        for k in FAR[n]:
+            j = lax.rem(own + k, n)
+            push(src(j), dst(own), ss.at[phase, k], rs.at[phase, own], dev(j))
 
     def finish(axis, phase, dst):
-        n, me, dev, ss, rs = axes[axis]
-        for k in range(1, n):
-            j = lax.rem(me + k, n)
+        n, own, dev, ss, rs = axes[axis]
+        for k in FAR[n]:
+            j = lax.rem(own + k, n)
             remote(dst(j), dst(j), ss.at[phase, k], rs.at[phase, j], dev(j)).wait_recv()
 
     def swap(phase, src, dst):
@@ -176,11 +177,10 @@
 
     loads = [load(pre_hbm, pre, 0), load(gh_hbm, gh, 1), load(qt_hbm, qt, 2)]
     barrier = pltpu.get_barrier_semaphore()
-    for axis in "zyx":
-        n, me, dev = axes[axis][:3]
-        for k in range(1, n):
-            pl.semaphore_signal(barrier, inc=1, device_id=dev(lax.rem(me + k, n)), device_id_type=MESH)
-    pl.semaphore_signal(barrier, inc=1, device_id=at(y, x, o, z), device_id_type=MESH)
+    for axis in "zyq":
+        n, own, dev = axes[axis][:3]
+        for k in FAR[n]:
+            pl.semaphore_signal(barrier, inc=1, device_id=dev(lax.rem(own + k, n)), device_id_type=MESH)
     eye = (lax.broadcasted_iota(jnp.int32, (R, R), 0) == lax.broadcasted_iota(jnp.int32, (R, R), 1)).astype(F32)
 
     loads[0].wait()
@@ -199,7 +199,7 @@
     lax.fori_loop(0, TOK // 32, activate, 0)
     loads[2].wait()
     h_part[...] = pair_rows(dot_wide(qt[...], g[...], NT).reshape(NZ, 8, TOK)).astype(BF16)
-    pl.semaphore_wait(barrier, 14)
+    pl.semaphore_wait(barrier, 17)
     start("z", 0, lambda j: h_part.at[j], lambda i: h_rs.at[i])
     h_rs[z] = h_part[z]
     w_loads[0].wait()
@@ -213,14 +213,15 @@
         return carry
 
     lax.fori_loop(0, NZ, error_rows, 0)
-    swap(0, pe_part.at[o], pe_c)
+    pe_send[...] = pe_part[o].reshape(NX, R, FEAT).astype(BF16)
+    swap(0, pe_send, pe_c)
     w_loads[1].wait()
     product(order[1])
     w_loads[2].wait()
     product(order[2])
     advance(SENDS["b"])
     swapped(0, pe_c)
-    pe_c[...] += pe_part[c]
+    pe_c[...] = (pe_c[...].astype(F32) + pe_part[c].reshape(NX, R, FEAT)).astype(BF16)
     start("x", 0, lambda j: pe_c.at[j], lambda i: pe_x.at[i])
     pe_x[x] = pe_c[x]
     finish("z", 0, lambda i: h_rs.at[i])
@@ -236,43 +237,39 @@
 
     lax.fori_loop(0, 5, products, 0)
     finish("x", 0, lambda i: pe_x.at[i])
-    pe_x[x] = pe_x[0] + pe_x[1] + pe_x[2] + pe_x[3]
-    start("z", 2, lambda j: pe_x.at[x, j], lambda i: pe_z.at[i])
-    pe_z[z] = pe_x[x, z]
+    pe_s[...] = jnp.sum(pe_x[...].astype(F32), axis=0).reshape(NZ, 8, FEAT)
+    start("z", 2, lambda j: pe_s.at[j], lambda i: pe_z.at[i])
+    pe_z[z] = pe_s[z]
     x_load.wait()
     advance(SENDS["d"])
     finish("z", 1, lambda i: h_ag.at[i])
     h_all = unpair_rows(h_ag[...].astype(F32)).reshape(R, TOK).astype(BF16)
-    px_part[...] = dot(h_all, xt[...], NT).reshape(2, NX, 8, FEAT)
-    swap(1, px_part.at[o], px_c)
+    px_part[...] = dot(h_all, xt[...], NT).reshape(2 * NX, 8, FEAT)
+    start("q", 0, lambda j: px_part.at[j], lambda i: px_rs.at[i])
+    px_rs[me] = px_part[me]
     advance(SENDS["e"])
-    swapped(1, px_c)
-    px_c[...] += px_part[c]
-    start("x", 1, lambda j: px_c.at[j], lambda i: px_x.at[i])
-    px_x[x] = px_c[x]
     advance(SENDS["f"])
     finish("z", 2, lambda i: pe_z.at[i])
     pe_sum = jnp.sum(pe_z[...], axis=0)
-    finish("x", 1, lambda i: px_x.at[i])
-    px_y[y] = jnp.sum(px_x[...], axis=0) + pe_sum
+    finish("q", 0, lambda i: px_rs.at[i])
+    px_y[y] = jnp.sum(px_rs[...], axis=0) + pe_sum
     start("y", 0, lambda j: px_y.at[y], lambda i: px_y.at[i])
     advance(SENDS["g"])
     finish("y", 0, lambda i: px_y.at[i])
     p_row = jnp.sum(px_y[...], axis=0)
-    pt[c, x] = p_row
-    pf[c, x, z] = p_row
-    start("x", 2, lambda j: pt.at[c, x], lambda i: pt.at[c, i])
-    start("z", 3, lambda j: pf.at[c, x, z], lambda i: pf.at[c, x, i])
+    pt[me] = p_row
+    pf_row[z] = p_row
+    start("q", 1, lambda j: pt.at[me], lambda i: pt.at[i])
+    start("z", 3, lambda j: pf_row.at[z], lambda i: pf_row.at[i])
     advance(SENDS["h"])
-    finish("x", 2, lambda i: pt.at[c, i])
-    swap(2, pt.at[c], pt.at[c])
-    swapped(2, pt.at[o])
+    finish("q", 1, lambda i: pt.at[i])
     z_sum = dot_wide(pt[...].reshape(R, FEAT), xt[...], NN).reshape(NZ, 8, TOK)
     z_part[...] = pair_rows(z_sum).astype(BF16)
     start("z", 4, lambda j: z_part.at[j], lambda i: z_rs.at[i])
     z_rs[z] = z_part[z]
     advance(SENDS["i"])
-    finish("z", 3, lambda i: pf.at[c, x, i])
+    finish("z", 3, lambda i: pf_row.at[i])
+    pf[c, x] = pf_row[...].reshape(R, FEAT).astype(BF16)
     start("x", 3, lambda j: pf.at[c, x], lambda i: pf.at[c, i])
     advance(SENDS["j"])
     finish("z", 4, lambda i: z_rs.at[i])
@@ -283,14 +280,17 @@
     swap(3, pf.at[c], pf.at[c])
     swapped(3, pf.at[o])
 
-    def features(t, gram):
-        rows = pf[:, :, t].reshape(R, FEAT)
-        y_err[...] += dot_wide(rows, eb[block(t), :], NN)
-        return gram + lax.dot_general(rows, rows, NT, precision=highest, preferred_element_type=F32)
-
+    def features(t, carry):
+        y_err[...] += dot(p_wide[:, t].reshape(R, FEAT).astype(BF16), eb[block(t), :], NN)
+        return carry
+
+    def squares(t, gram):
+        rows = p_wide[:, t].reshape(R, FEAT).astype(BF16)
+        return gram + dot(rows, rows, NT)
+
+    p_wide[...] = pf[...].astype(F32).reshape(2 * NX, NZ, 8, FEAT)
     y_err[...] = jnp.zeros_like(y_err)
-    gram = lax.fori_loop(0, NZ, features, jnp.zeros((R, R), F32))
-    work[...] = jnp.concatenate([gram, eye], axis=1)
+    lax.fori_loop(0, NZ, features, 0)
     advance(SENDS["l"])
     drain()
     finish("z", 5, lambda i: z_ag.at[i])
@@ -298,27 +298,28 @@
     y_part[...] = (y_err[...] + dot(z_all, g[...], NN)).reshape(2, NX, 8, HID)
     swap(4, y_part.at[o], y_c)
     advance(SENDS["m"])
-    eliminate(work, 0, 8, z >= 0)
     swapped(4, y_c)
     y_c[...] += y_part[c]
     start("x", 4, lambda j: y_c.at[j], lambda i: y_x.at[i])
     y_x[x] = y_c[x]
     advance(SENDS["n"])
-    eliminate(work, 8, 24, z >= 0)
+    gram = lax.fori_loop(0, NZ, squares, jnp.zeros((R, R), F32))
+    work[...] = jnp.concatenate([gram, eye], axis=1)
+    eliminate(work, 0, 14, z >= 0)
     finish("x", 4, lambda i: y_x.at[i])
     y_y[y] = jnp.sum(y_x[...], axis=0)
     start("y", 1, lambda j: y_y.at[y], lambda i: y_y.at[i])
     advance(SENDS["o"])
-    eliminate(work, 24, 40, z >= 0)
+    eliminate(work, 14, 36, z >= 0)
     finish("y", 1, lambda i: y_y.at[i])
     y_f[c, x] = jnp.sum(y_y[...], axis=0)
     start("x", 5, lambda j: y_f.at[c, x], lambda i: y_f.at[c, i])
     advance(SENDS["p"])
-    eliminate(work, 40, 56, z >= 0)
+    eliminate(work, 36, 58, z >= 0)
     finish("x", 5, lambda i: y_f.at[c, i])
     swap(5, y_f.at[c], y_f.at[c])
     advance(SENDS["q"])
-    eliminate(work, 56, 64, z >= 0)
+    eliminate(work, 58, 64, z >= 0)
     diag = jnp.sum(work[:, :R] * eye, axis=1, keepdims=True)
     inverse = work[:, R:] * (lax.rsqrt(diag) * (1.0 / (NX * NY * 2)))
     advance(len(todo))
@@ -336,41 +337,29 @@
     drain()
 
 
-def deliver(q_ref, gi_ref, q_out, gi_out):
-    q_out[...] = q_ref[...]
-    gi_out[...] = gi_ref[...]
-
-
 def local(tokens, w_in, pre_act, grad_hidden, err_state, q_init):
     vm = lambda *shape: pltpu.VMEM(shape, F32)
     vb = lambda *shape: pltpu.VMEM(shape, BF16)
     dma = pltpu.SemaphoreType.DMA
     q_factor, grad_input = pl.pallas_call(
         kernel,
-        out_shape=[jax.ShapeDtypeStruct((R, HID), F32), jax.ShapeDtypeStruct((FEAT, TOK), BF16)],
+        out_shape=[vm(R, HID), vb(FEAT, TOK)],
         in_specs=[pl.BlockSpec(memory_space=pl.ANY)] * 6,
         out_specs=[pl.BlockSpec(memory_space=pltpu.VMEM)] * 2,
         scratch_shapes=[vb(TOK, HID), vb(TOK, HID), vm(R, HID), vb(NZ * FEAT, HID), vm(NZ * FEAT, HID),
                         vb(FEAT, TOK), vb(TOK, HID), vb(NZ * FEAT, HID), vb(NZ, FEAT, TOK), vb(2, 7, NCH, CHUNK, TOK)]
         + [vb(NZ, 16, TOK // 2)] * 6
-        + [vm(2, NX, 8, FEAT), vm(NX, 8, FEAT), vm(NX, 8, FEAT), vm(NY, 8, FEAT), vm(2, NX, 8, FEAT)]
-        + [vm(2, NX, NZ, 8, FEAT), vm(NX, NZ, 8, FEAT), vm(NX, NZ, 8, FEAT), vm(NZ, 8, FEAT), vm(2, NX, NZ, 8, FEAT)]
+        + [vm(2 * NX, 8, FEAT), vm(2 * NX, 8, FEAT), vm(NY, 8, FEAT), vm(2 * NX, 8, FEAT)]
+        + [vm(2, NX, NZ, 8, FEAT), vb(NX, R, FEAT), vb(NX, R, FEAT), vb(NX, R, FEAT), vm(NZ, 8, FEAT), vm(NZ, 8, FEAT),
+           vm(NZ, 8, FEAT), vb(2, NX, R, FEAT), vm(2 * NX, NZ, 8, FEAT)]
         + [vm(2, NX, 8, HID), vm(NX, 8, HID), vm(NX, 8, HID), vm(NY, 8, HID), vm(2, NX, 8, HID), vm(R, HID),
            vm(R, 2 * R)]
-        + [dma((6, NZ)), dma((6, NZ)), dma((6, NX)), dma((6, NX)), dma((2, NY)), dma((2, NY)), dma((6,)), dma((6,)),
+        + [dma((6, NZ)), dma((6, NZ)), dma((2, 2 * NX)), dma((2, 2 * NX)), dma((6, NX)), dma((6, NX)), dma((2, NY)), dma((2, NY)), dma((6,)), dma((6,)),
            dma((2, 7, NCH)), dma((2, 7, NCH)), dma((20,))],
         compiler_params=pltpu.CompilerParams(
             collective_id=0, has_side_effects=True, vmem_limit_bytes=56 << 20),
         name="backward",
     )(pre_act, grad_hidden, q_init.T, w_in, err_state[0], tokens.T)
-    q_factor, grad_input = pl.pallas_call(
-        deliver,
-        out_shape=[jax.ShapeDtypeStruct((R, HID), F32), jax.ShapeDtypeStruct((FEAT, TOK), BF16)],
-        in_specs=[pl.BlockSpec(memory_space=pltpu.VMEM)] * 2,
-        out_specs=[pl.BlockSpec(memory_space=pltpu.VMEM)] * 2,
-        compiler_params=pltpu.CompilerParams(vmem_limit_bytes=56 << 20),
-        name="deliver",
-    )(q_factor, grad_input)
     return (grad_input.T, q_factor.T)
 
 

time: 72.5 us -> 65.8 us (0.908)
  Pallas kernels: 71.7 us -> 63.6 us
  local copies, waits for them, and re-layouts: 0 us -> 1.45 us
    pallas_call x2 -> x1, Pallas kernels: 71.7 us -> 63.6 us  [local(): pl.pallas_call(kernel, out_shape=[vm(R, HID), vb(FEAT, TOK)], in_specs=[p...]
    unnamed x0 -> x2, local copies, waits for them, and re-layouts: none -> 1.45 us
where the time goes in v6:
time: 65.8 us; the launch traced here: 65.7 us
  Pallas kernels  63.6 us (97%)
  local copies, waits for them, and re-layouts  1.45 us (2%)
    pallas_call x1, Pallas kernels, local(): pl.pallas_call(kernel, out_shape=[vm(R, HID), vb(FEAT, TOK)], in_specs=[p...  63.6 us
    unnamed x2, local copies, waits for them, and re-layouts  1.45 us

profile of v6, /device:TPU:1, one launch (start us, length us, event | category | flops | bytes accessed | tf_op | source)
XLA Modules:
  0.0 65.7 jit_solution(4907231979481047402)
XLA Ops:
  0.6 63.6 %backward.1 = (f32[64,640]{1,0:T(8,128)S(1)}, bf16[320,768]{1,0:T(8,128)(2,1)S(1)}) custom-call(bf16[768,640]{1,0:T(8,128)(2,1)} %pre_hbm.1, bf16[768,640]{1,0:T(8,128)(2,1)} %gh_hbm.1, f32[64,640]{1,0:T(8,128)} %bitcast.9, bf16[2560,640]{1,0:T(8,128)(2,1)} %w_hbm.1, f32[2560,640]{1,0:T(8,128)} %bitcast.7, bf16[320,768]{1,0:T(8,128)(2,1)} %bitcast.8), custom_call_target="tpu_custom_call" | custom-call | tf_op jit(solution)/shard_map/backward/pallas_call | solution.py:344
  64.3 0.8 %copy.10 = bf16[768,320]{0,1:T(8,128)(2,1)} copy(bf16[768,320]{0,1:T(8,128)(2,1)S(1)} %bitcast.5) | data formatting | bytes 983040
  65.0 0.7 %copy.11 = f32[640,64]{0,1:T(8,128)} copy(f32[640,64]{0,1:T(8,128)S(1)} %bitcast.6) | data formatting | bytes 327680

commit v7 on v6

--- a/solution.py
+++ b/solution.py
@@ -14,7 +14,7 @@
 HALF = FEAT // 2
 CHUNK = HALF // NCH
 HOPS = (4, 3, 3, 2, 2, 1, 1)
-SENDS = dict(a=2, b=0, c=0, d=1, e=1, f=1, g=1, h=1, i=1, j=0, k=1, l=0, m=2, n=1, o=1, p=1, q=0)
+SENDS = dict(a=2, b=0, c=0, d=1, e=1, f=1, g=1, h=1, i=1, j=0, k=1, l=0, m=4, n=1, o=0, p=0, q=0)
 FAR = {4: (2, 1, 3), 8: (4, 3, 5, 2, 6, 1, 7)}
 NN = (((1,), (0,)), ((), ()))
 NT = (((1,), (1,)), ((), ()))
@@ -40,11 +40,6 @@
     rows = left.shape[0]
     both = dot(jnp.concatenate(halves(left), axis=0), right, dims)
     return both[:rows] + both[rows:]
-
-
-def dot_both(left, right, dims):
-    high, low = halves(right)
-    return dot_wide(left, high, dims) + dot(left.astype(BF16), low, dims)
 
 
 def pair_rows(value):
@@ -75,7 +70,7 @@
     h_part, h_rs, h_ag, z_part, z_rs, z_ag,
     px_part, px_rs, px_y, pt,
     pe_part, pe_send, pe_c, pe_x, pe_s, pe_z, pf_row, pf, p_wide,
-    y_part, y_c, y_x, y_y, y_f, y_err, work,
+    y_part, y_rs, y_y, y_f, y_err, work,
     s_z, r_z, s_q, r_q, s_x, r_x, s_y, r_y, s_c, r_c, s_g, r_g, s_in,
 ):
     dp, z = lax.axis_index("dp"), lax.axis_index("tensor")
@@ -175,12 +170,12 @@
     def load_e(t):
         return pltpu.make_async_copy(e_hbm.at[block(t)], e.at[block(t)], s_in.at[12 + t])
 
-    loads = [load(pre_hbm, pre, 0), load(gh_hbm, gh, 1), load(qt_hbm, qt, 2)]
     barrier = pltpu.get_barrier_semaphore()
     for axis in "zyq":
         n, own, dev = axes[axis][:3]
         for k in FAR[n]:
             pl.semaphore_signal(barrier, inc=1, device_id=dev(lax.rem(own + k, n)), device_id_type=MESH)
+    loads = [load(pre_hbm, pre, 0), load(gh_hbm, gh, 1), load(qt_hbm, qt, 2)]
     eye = (lax.broadcasted_iota(jnp.int32, (R, R), 0) == lax.broadcasted_iota(jnp.int32, (R, R), 1)).astype(F32)
 
     loads[0].wait()
@@ -199,11 +194,11 @@
     lax.fori_loop(0, TOK // 32, activate, 0)
     loads[2].wait()
     h_part[...] = pair_rows(dot_wide(qt[...], g[...], NT).reshape(NZ, 8, TOK)).astype(BF16)
+    w_loads[0].wait()
+    product(order[0])
     pl.semaphore_wait(barrier, 17)
     start("z", 0, lambda j: h_part.at[j], lambda i: h_rs.at[i])
     h_rs[z] = h_part[z]
-    w_loads[0].wait()
-    product(order[0])
     advance(SENDS["a"])
 
     def error_rows(t, carry):
@@ -237,7 +232,7 @@
 
     lax.fori_loop(0, 5, products, 0)
     finish("x", 0, lambda i: pe_x.at[i])
-    pe_s[...] = jnp.sum(pe_x[...].astype(F32), axis=0).reshape(NZ, 8, FEAT)
+    pe_s[...] = pair_rows(jnp.sum(pe_x[...].astype(F32), axis=0).reshape(NZ, 8, FEAT)).astype(BF16)
     start("z", 2, lambda j: pe_s.at[j], lambda i: pe_z.at[i])
     pe_z[z] = pe_s[z]
     x_load.wait()
@@ -250,7 +245,7 @@
     advance(SENDS["e"])
     advance(SENDS["f"])
     finish("z", 2, lambda i: pe_z.at[i])
-    pe_sum = jnp.sum(pe_z[...], axis=0)
+    pe_sum = unpair_rows(jnp.sum(pe_z[...].astype(F32), axis=0))
     finish("q", 0, lambda i: px_rs.at[i])
     px_y[y] = jnp.sum(px_rs[...], axis=0) + pe_sum
     start("y", 0, lambda j: px_y.at[y], lambda i: px_y.at[i])
@@ -258,7 +253,7 @@
     finish("y", 0, lambda i: px_y.at[i])
     p_row = jnp.sum(px_y[...], axis=0)
     pt[me] = p_row
-    pf_row[z] = p_row
+    pf_row[z] = pair_rows(p_row).astype(BF16)
     start("q", 1, lambda j: pt.at[me], lambda i: pt.at[i])
     start("z", 3, lambda j: pf_row.at[z], lambda i: pf_row.at[i])
     advance(SENDS["h"])
@@ -269,7 +264,7 @@
     z_rs[z] = z_part[z]
     advance(SENDS["i"])
     finish("z", 3, lambda i: pf_row.at[i])
-    pf[c, x] = pf_row[...].reshape(R, FEAT).astype(BF16)
+    pf[c, x] = unpair_rows(pf_row[...].astype(F32)).reshape(R, FEAT).astype(BF16)
     start("x", 3, lambda j: pf.at[c, x], lambda i: pf.at[c, i])
     advance(SENDS["j"])
     finish("z", 4, lambda i: z_rs.at[i])
@@ -295,31 +290,26 @@
     drain()
     finish("z", 5, lambda i: z_ag.at[i])
     z_all = unpair_rows(z_ag[...].astype(F32)).reshape(R, TOK).astype(BF16)
-    y_part[...] = (y_err[...] + dot(z_all, g[...], NN)).reshape(2, NX, 8, HID)
-    swap(4, y_part.at[o], y_c)
+    y_sum = (y_err[...] + dot(z_all, g[...], NN)).reshape(2 * NX, 8, HID)
+    y_part[...] = pair_rows(y_sum).astype(BF16)
+    start("q", 2, lambda j: y_part.at[j], lambda i: y_rs.at[i])
+    y_rs[me] = y_part[me]
     advance(SENDS["m"])
-    swapped(4, y_c)
-    y_c[...] += y_part[c]
-    start("x", 4, lambda j: y_c.at[j], lambda i: y_x.at[i])
-    y_x[x] = y_c[x]
-    advance(SENDS["n"])
     gram = lax.fori_loop(0, NZ, squares, jnp.zeros((R, R), F32))
     work[...] = jnp.concatenate([gram, eye], axis=1)
-    eliminate(work, 0, 14, z >= 0)
-    finish("x", 4, lambda i: y_x.at[i])
-    y_y[y] = jnp.sum(y_x[...], axis=0)
+    eliminate(work, 0, 18, z >= 0)
+    finish("q", 2, lambda i: y_rs.at[i])
+    y_y[y] = jnp.sum(y_rs[...].astype(F32), axis=0).astype(BF16)
     start("y", 1, lambda j: y_y.at[y], lambda i: y_y.at[i])
+    advance(SENDS["n"])
     advance(SENDS["o"])
-    eliminate(work, 14, 36, z >= 0)
+    eliminate(work, 18, 40, z >= 0)
     finish("y", 1, lambda i: y_y.at[i])
-    y_f[c, x] = jnp.sum(y_y[...], axis=0)
-    start("x", 5, lambda j: y_f.at[c, x], lambda i: y_f.at[c, i])
+    y_f[me] = jnp.sum(y_y[...].astype(F32), axis=0).astype(BF16)
+    start("q", 3, lambda j: y_f.at[me], lambda i: y_f.at[i])
     advance(SENDS["p"])
-    eliminate(work, 36, 58, z >= 0)
-    finish("x", 5, lambda i: y_f.at[c, i])
-    swap(5, y_f.at[c], y_f.at[c])
     advance(SENDS["q"])
-    eliminate(work, 58, 64, z >= 0)
+    eliminate(work, 40, 64, z >= 0)
     diag = jnp.sum(work[:, :R] * eye, axis=1, keepdims=True)
     inverse = work[:, R:] * (lax.rsqrt(diag) * (1.0 / (NX * NY * 2)))
     advance(len(todo))
@@ -332,8 +322,9 @@
             rows = pl.ds(half * HALF + ch * CHUNK, CHUNK)
             long, short = ring[half, 6, ch].astype(F32), ring[1 - half, 5, ch].astype(F32)
             gi_out[rows, :] = (part[z, rows].astype(F32) + long + short).astype(BF16)
-    swapped(5, y_f.at[o])
-    q_out[...] = dot_both(inverse, y_f[...].reshape(R, HID), NN)
+    finish("q", 3, lambda i: y_f.at[i])
+    y_all = unpair_rows(y_f[...].astype(F32)).reshape(R, HID).astype(BF16)
+    q_out[...] = dot_wide(inverse, y_all, NN)
     drain()
 
 
@@ -350,11 +341,11 @@
                         vb(FEAT, TOK), vb(TOK, HID), vb(NZ * FEAT, HID), vb(NZ, FEAT, TOK), vb(2, 7, NCH, CHUNK, TOK)]
         + [vb(NZ, 16, TOK // 2)] * 6
         + [vm(2 * NX, 8, FEAT), vm(2 * NX, 8, FEAT), vm(NY, 8, FEAT), vm(2 * NX, 8, FEAT)]
-        + [vm(2, NX, NZ, 8, FEAT), vb(NX, R, FEAT), vb(NX, R, FEAT), vb(NX, R, FEAT), vm(NZ, 8, FEAT), vm(NZ, 8, FEAT),
-           vm(NZ, 8, FEAT), vb(2, NX, R, FEAT), vm(2 * NX, NZ, 8, FEAT)]
-        + [vm(2, NX, 8, HID), vm(NX, 8, HID), vm(NX, 8, HID), vm(NY, 8, HID), vm(2, NX, 8, HID), vm(R, HID),
+        + [vm(2, NX, NZ, 8, FEAT), vb(NX, R, FEAT), vb(NX, R, FEAT), vb(NX, R, FEAT), vb(NZ, 16, FEAT // 2), vb(NZ, 16, FEAT // 2),
+           vb(NZ, 16, FEAT // 2), vb(2, NX, R, FEAT), vm(2 * NX, NZ, 8, FEAT)]
+        + [vb(2 * NX, 16, HID // 2), vb(2 * NX, 16, HID // 2), vb(NY, 16, HID // 2), vb(2 * NX, 16, HID // 2), vm(R, HID),
            vm(R, 2 * R)]
-        + [dma((6, NZ)), dma((6, NZ)), dma((2, 2 * NX)), dma((2, 2 * NX)), dma((6, NX)), dma((6, NX)), dma((2, NY)), dma((2, NY)), dma((6,)), dma((6,)),
+        + [dma((6, NZ)), dma((6, NZ)), dma((4, 2 * NX)), dma((4, 2 * NX)), dma((6, NX)), dma((6, NX)), dma((2, NY)), dma((2, NY)), dma((6,)), dma((6,)),
            dma((2, 7, NCH)), dma((2, 7, NCH)), dma((20,))],
         compiler_params=pltpu.CompilerParams(
             collective_id=0, has_side_effects=True, vmem_limit_bytes=56 << 20),

time: 65.8 us -> 65.2 us (level)
  Pallas kernels: 63.6 us -> 62.5 us
    pallas_call x1, Pallas kernels: 63.6 us -> 62.5 us  [local(): pl.pallas_call(kernel, out_shape=[vm(R, HID), vb(FEAT, TOK)], in_specs=[p...]
where the time goes in v7:
time: 65.2 us; the launch traced here: 64.6 us
  Pallas kernels  62.5 us (96%)
  local copies, waits for them, and re-layouts  1.45 us (2%)
    pallas_call x1, Pallas kernels, local(): pl.pallas_call(kernel, out_shape=[vm(R, HID), vb(FEAT, TOK)], in_specs=[p...  62.5 us
    unnamed x2, local copies, waits for them, and re-layouts  1.45 us

profile of v7, /device:TPU:1, one launch (start us, length us, event | category | flops | bytes accessed | tf_op | source)
XLA Modules:
  0.0 64.6 jit_solution(3863917516992850620)
XLA Ops:
  0.6 62.5 %backward.1 = (f32[64,640]{1,0:T(8,128)S(1)}, bf16[320,768]{1,0:T(8,128)(2,1)S(1)}) custom-call(bf16[768,640]{1,0:T(8,128)(2,1)} %pre_hbm.1, bf16[768,640]{1,0:T(8,128)(2,1)} %gh_hbm.1, f32[64,640]{1,0:T(8,128)} %bitcast.9, bf16[2560,640]{1,0:T(8,128)(2,1)} %w_hbm.1, f32[2560,640]{1,0:T(8,128)} %bitcast.7, bf16[320,768]{1,0:T(8,128)(2,1)} %bitcast.8), custom_call_target="tpu_custom_call" | custom-call | tf_op jit(solution)/shard_map/backward/pallas_call | solution.py:335
  63.2 0.8 %copy.10 = bf16[768,320]{0,1:T(8,128)(2,1)} copy(bf16[768,320]{0,1:T(8,128)(2,1)S(1)} %bitcast.5) | data formatting | bytes 983040
  64.0 0.7 %copy.11 = f32[640,64]{0,1:T(8,128)} copy(f32[640,64]{0,1:T(8,128)S(1)} %bitcast.6) | data formatting | bytes 327680
